TPU v7x, 512 devices: a whole 4x4x16 slice. The times are simulated.
512 devices in a mesh: blk: 128 (over x_hi, z, y), fld: 4 (over x_lo, core).
Axes of the slice: x: 4 (x_hi: 2, x_lo: 2; x = x_hi * 2 + x_lo), y: 4, z: 16, core: 2. Of those that a mesh axis runs over, the one named last changes fastest.
Arguments:
- coef: bfloat16 [1024, 1280, 256], P(('blk', 'fld')), may hold values from -6 to 6
- leg: bfloat16 [1024, 256, 1280], P(('blk', 'fld')), may hold values from -0.15625 to 0.15625
- vcoef: float32 [4, 7, 32], P('fld'), may hold values from -2.4 to 2.4
- obs_value: bfloat16 [4, 32, 65536], P('fld', None, 'blk'), may hold values from -6 to 6
- obs_weight: float32 [4, 32, 65536], P('fld', None, 'blk'), may hold values from 1 to 10
- obs_dest: int32 [65536, 1], P('blk'), may hold values from 0 to 127; in each aligned block of 512 rows (0 to 511, 512 to 1023, ...) at most 6 rows name the same one
- obs_spot: int32 [65536], P('blk'), may hold values from 0 to 5119
- obs_count: int32 [128], P('blk'), may hold values from 1 to 512, 49280 in all
Outputs:
- obs_gradient: bfloat16 [1024, 1280, 256], P(('blk', 'fld'))
Inputs may be any that keep to these rules, and one draw needn't show every extreme that they name: `obs_dest`: in the rows of one index of blk, no band is named more than 6 times, a bound that some block reaches. `obs_count`: some list is full.
All inputs are finite; a program needn't handle non-finite values. No bound on the sum of `obs_count` on one device may be relied on, other than what follows from the above.
Results may differ from a plain program's by a relative error of at most 0.0085.
Values may be sent and summed in bfloat16 or wider, within the bound.
A program may use at most 64 MiB of HBM per device.

v0:
```python
import math

import jax
import jax.numpy as jnp
from jax import lax
from jax.sharding import PartitionSpec as P

NLON = 2560


def zonal_table(start, count, waves, nlon):
    wave_ids = jnp.arange(waves, dtype=jnp.int32)
    longitude = start + jnp.arange(count, dtype=jnp.int32)
    phase = wave_ids[:, None] * longitude[None, :] % nlon
    angle = phase.astype(jnp.float32) * (2.0 * math.pi / nlon)
    both = jnp.stack([jnp.cos(angle), jnp.sin(angle)], axis=1)
    return both.reshape(2 * waves, count).astype(jnp.bfloat16)


def vertical(grid, coefs, levels, half):
    padded = jnp.pad(grid, ((0, 0), (half, half), (0, 0)))
    total = jnp.zeros(grid.shape, jnp.float32)
    for shift in range(2 * half + 1):
        total = total + coefs[:, shift, :, None] * padded[:, shift : shift + levels, :]
    return total


def vertical_adjoint(field, coefs, levels, half):
    total = jnp.zeros(field.shape, jnp.float32)
    for shift in range(2 * half + 1):
        term = coefs[:, shift, :, None] * field
        padded = jnp.pad(term, ((0, 0), (half, half), (0, 0)))
        begin = 2 * half - shift
        total = total + padded[:, begin : begin + levels, :]
    return total


def on_device(coef, leg, vcoef, obs_value, obs_weight, obs_dest, obs_spot, obs_count):
    local_waves, total_waves = (coef.shape[0], coef.shape[1])
    nblk = lax.axis_size("blk")
    nfld = lax.axis_size("fld")
    levels = vcoef.shape[2]
    fields = vcoef.shape[0] * nfld
    lat_all = leg.shape[1]
    lat_dev = lat_all // nblk
    waves = local_waves * nblk * nfld
    half = (vcoef.shape[1] - 1) // 2
    nlon = NLON
    block = 256
    scale = 1.0 / math.sqrt(waves)
    four = jnp.einsum("mjn,mnc->mjc", leg, coef, preferred_element_type=jnp.float32).astype(
        jnp.bfloat16
    )
    four = four.reshape(1, local_waves, lat_all, 2, fields, levels)
    bands = lax.all_to_all(
        lax.all_to_all(four, "blk", split_axis=2, concat_axis=0, tiled=True),
        "fld",
        split_axis=4,
        concat_axis=1,
        tiled=True,
    )
    bands = bands.reshape(waves, lat_dev, 2, levels)
    rows = jnp.transpose(bands, (1, 3, 0, 2)).reshape(lat_dev * levels, 2 * waves)

    def forward_block(which):
        table = zonal_table(which * block, block, waves, nlon)
        return jnp.dot(rows, table, preferred_element_type=jnp.float32)

    pieces = lax.map(forward_block, jnp.arange(nlon // block, dtype=jnp.int32))
    grid = jnp.transpose(pieces, (1, 0, 2)).reshape(lat_dev, levels, nlon) * scale
    incr = vertical(grid, vcoef, levels, half)
    obs_dev = obs_spot.shape[0]
    cap = 3 * obs_dev // (2 * nblk)
    slots = nblk * cap
    dest = obs_dest[:, 0]
    onehot_dest = (dest[:, None] == jnp.arange(nblk, dtype=jnp.int32)[None, :]).astype(jnp.float32)
    order = jnp.arange(obs_dev, dtype=jnp.int32)
    earlier = (order[:, None] > order[None, :]).astype(jnp.float32)
    before = jnp.dot(earlier, onehot_dest, precision=lax.Precision.HIGHEST)
    rank = jnp.sum(before * onehot_dest, axis=1).astype(jnp.int32)
    slot = dest * cap + rank
    live = order < obs_count[0]
    select = (
        (slot[:, None] == jnp.arange(slots, dtype=jnp.int32)[None, :]) & live[:, None]
    ).astype(jnp.float32)
    sent_values = jnp.dot(obs_value[0].astype(jnp.float32), select, precision=lax.Precision.HIGHEST)
    sent_weights = jnp.dot(obs_weight[0], select, precision=lax.Precision.HIGHEST)
    sent_spots = jnp.dot(
        obs_spot.astype(jnp.float32)[None, :], select, precision=lax.Precision.HIGHEST
    )
    columns = jnp.transpose(incr, (1, 0, 2)).reshape(levels, lat_dev * nlon)
    asked = lax.all_to_all(
        sent_spots.astype(jnp.int32), "blk", split_axis=1, concat_axis=1, tiled=True
    )
    spot_in = asked[0]
    found = jnp.take(columns, spot_in, axis=1)
    model = lax.all_to_all(found, "blk", split_axis=1, concat_axis=1, tiled=True)
    mine = sent_weights * (model - sent_values)
    weighted = lax.all_to_all(mine, "blk", split_axis=1, concat_axis=1, tiled=True)
    summed = jax.ops.segment_sum(weighted.T, spot_in, num_segments=lat_dev * nlon)
    adjoint = jnp.transpose(summed.T.reshape(levels, lat_dev, nlon), (1, 0, 2))
    back = vertical_adjoint(adjoint, vcoef, levels, half).astype(jnp.bfloat16)
    back_rows = back.reshape(lat_dev * levels, nlon)

    def adjoint_block(which, total):
        table = zonal_table(which * block, block, waves, nlon)
        piece = lax.dynamic_slice_in_dim(back_rows, which * block, block, 1)
        return total + lax.dot_general(
            table, piece, (((1,), (1,)), ((), ())), preferred_element_type=jnp.float32
        )

    spectral = lax.fori_loop(
        0, nlon // block, adjoint_block, jnp.zeros((2 * waves, lat_dev * levels), jnp.float32)
    )
    wave = (spectral * scale).astype(jnp.bfloat16).reshape(waves, 2, lat_dev, levels)
    wave = jnp.transpose(wave, (0, 2, 1, 3)).reshape(
        nblk, nfld * local_waves, lat_dev, 2, 1, levels
    )
    home = lax.all_to_all(
        lax.all_to_all(wave, "blk", split_axis=0, concat_axis=2, tiled=True),
        "fld",
        split_axis=1,
        concat_axis=4,
        tiled=True,
    )
    home = home.reshape(local_waves, lat_all, 2 * fields * levels)
    result = jnp.einsum("mjn,mjc->mnc", leg, home, preferred_element_type=jnp.float32).astype(
        jnp.bfloat16
    )
    return result


def solution(mesh):
    in_specs = (
        P(("blk", "fld"), None, None),
        P(("blk", "fld"), None, None),
        P("fld", None, None),
        P("fld", None, "blk"),
        P("fld", None, "blk"),
        P("blk", None),
        P("blk"),
        P("blk"),
    )
    out_specs = P(("blk", "fld"), None, None)
    return jax.shard_map(
        on_device, mesh=mesh, in_specs=in_specs, out_specs=out_specs, check_vma=False
    )
```

profile of v0, /device:TPU:1, one launch (start us, length us, event | category | flops | bytes accessed | tf_op | source)
XLA Modules:
  0.0 394.4 jit_solution(15973212080023682712)
XLA Ops:
  4.6 23.0 %all-to-all-start = ((s32[1,128,6]{2,0,1:T(1,128)}), s32[1,128,6]{2,0,1:T(1,128)S(1)}, u32[]{:S(2)}, u32[]{:S(2)}) async-start(s32[1,128,6]{2,0,1:T(1,128)} %bitcast.9), calls=%async_computation | async-start | bytes 131072 | tf_op jit(solution)/shard_map/all_to_all | solution.py:92
  32.0 11.5 %all-to-all-done = s32[1,128,6]{2,0,1:T(1,128)S(1)} async-done(((s32[1,128,6]{2,0,1:T(1,128)}), s32[1,128,6]{2,0,1:T(1,128)S(1)}, u32[]{:S(2)}, u32[]{:S(2)}) %all-to-all-start) | async-done | bytes 3104 | tf_op jit(solution)/shard_map/all_to_all | solution.py:92
  43.5 6.7 %all-to-all-start.1 = ((bf16[128,2,512]{2,1,0:T(2,128)(2,1)}), bf16[128,2,512]{2,1,0:T(2,128)(2,1)S(1)}, u32[]{:S(2)}, u32[]{:S(2)}) async-start(bf16[128,2,512]{2,1,0:T(2,128)(2,1)} %reshape.338), calls=%async_computation.1 | async-start | bytes 524288 | tf_op jit(solution)/shard_map/all_to_all | solution.py:56
  50.4 22.3 %all-to-all-done.1 = bf16[128,2,512]{2,1,0:T(2,128)(2,1)S(1)} async-done(((bf16[128,2,512]{2,1,0:T(2,128)(2,1)}), bf16[128,2,512]{2,1,0:T(2,128)(2,1)S(1)}, u32[]{:S(2)}, u32[]{:S(2)}) %all-to-all-start.1) | async-done | bytes 262176 | tf_op jit(solution)/shard_map/all_to_all | solution.py:56
  75.2 7.3 %all-to-all-start.2 = ((bf16[128,2,2,2,4,32]{0,5,3,2,1,4:T(8,128)(2,1)}), bf16[128,2,2,2,4,32]{0,5,3,2,1,4:T(8,128)(2,1)S(1)}, u32[]{:S(2)}, u32[]{:S(2)}) async-start(bf16[128,2,2,2,4,32]{0,5,3,2,1,4:T(8,128)(2,1)} %copy.85), calls=%async_computation.2 | async-start | bytes 524288 | tf_op jit(solution)/shard_map/all_to_all | solution.py:55
  82.5 5.1 %all-to-all-done.2 = bf16[128,2,2,2,4,32]{0,5,3,2,1,4:T(8,128)(2,1)S(1)} async-done(((bf16[128,2,2,2,4,32]{0,5,3,2,1,4:T(8,128)(2,1)}), bf16[128,2,2,2,4,32]{0,5,3,2,1,4:T(8,128)(2,1)S(1)}, u32[]{:S(2)}, u32[]{:S(2)}) %all-to-all-start.2) | async-done | bytes 262176 | tf_op jit(solution)/shard_map/all_to_all | solution.py:55
  90.9 93.4 %while.28 = (s32[]{:T(128)}, f32[10,64,256]{2,1,0:T(8,128)}, s32[10]{0:T(128)S(1)}, bf16[64,2048]{1,0:T(8,128)(2,1)}, s32[]{:T(128)}, /*index=5*/s32[1]{0:T(128)}) while((s32[]{:T(128)}, f32[10,64,256]{2,1,0:T(8,128)}, s32[10]{0:T(128)S(1)}, bf16[64,2048]{1,0:T(8,128)(2,1)}, s32[]{:T(128)}, /*index=5*/s32[1]{0:T(128)}) %tuple.83), condition=%wide.region_2.3_spmd, body=%wide.region_1.2_spmd.sunk | while | flops 70516992 | bytes 8718945 | solution.py:69
  92.2 4.6 %cosine_convert_fusion.4 = (bf16[1024,1,256]{2,0,1:T(8,128)(2,1)S(1)}, bf16[1024,1,256]{2,0,1:T(8,128)(2,1)S(1)}) fusion(s32[256]{0:T(256)S(1)} %iota_add_fusion.4), kind=kLoop, calls=%fused_computation.9.clone.1 | loop fusion | flops 2883584 | bytes 1049600 | tf_op jit(solution)/shard_map/convert
  101.5 4.6 %cosine_convert_fusion.4 = (bf16[1024,1,256]{2,0,1:T(8,128)(2,1)S(1)}, bf16[1024,1,256]{2,0,1:T(8,128)(2,1)S(1)}) fusion(s32[256]{0:T(256)S(1)} %iota_add_fusion.4), kind=kLoop, calls=%fused_computation.9.clone.1 | loop fusion | flops 2883584 | bytes 1049600 | tf_op jit(solution)/shard_map/convert
  110.8 4.6 %cosine_convert_fusion.4 = (bf16[1024,1,256]{2,0,1:T(8,128)(2,1)S(1)}, bf16[1024,1,256]{2,0,1:T(8,128)(2,1)S(1)}) fusion(s32[256]{0:T(256)S(1)} %iota_add_fusion.4), kind=kLoop, calls=%fused_computation.9.clone.1 | loop fusion | flops 2883584 | bytes 1049600 | tf_op jit(solution)/shard_map/convert
  120.2 4.6 %cosine_convert_fusion.4 = (bf16[1024,1,256]{2,0,1:T(8,128)(2,1)S(1)}, bf16[1024,1,256]{2,0,1:T(8,128)(2,1)S(1)}) fusion(s32[256]{0:T(256)S(1)} %iota_add_fusion.4), kind=kLoop, calls=%fused_computation.9.clone.1 | loop fusion | flops 2883584 | bytes 1049600 | tf_op jit(solution)/shard_map/convert
  129.5 4.6 %cosine_convert_fusion.4 = (bf16[1024,1,256]{2,0,1:T(8,128)(2,1)S(1)}, bf16[1024,1,256]{2,0,1:T(8,128)(2,1)S(1)}) fusion(s32[256]{0:T(256)S(1)} %iota_add_fusion.4), kind=kLoop, calls=%fused_computation.9.clone.1 | loop fusion | flops 2883584 | bytes 1049600 | tf_op jit(solution)/shard_map/convert
  138.9 4.6 %cosine_convert_fusion.4 = (bf16[1024,1,256]{2,0,1:T(8,128)(2,1)S(1)}, bf16[1024,1,256]{2,0,1:T(8,128)(2,1)S(1)}) fusion(s32[256]{0:T(256)S(1)} %iota_add_fusion.4), kind=kLoop, calls=%fused_computation.9.clone.1 | loop fusion | flops 2883584 | bytes 1049600 | tf_op jit(solution)/shard_map/convert
  148.2 4.6 %cosine_convert_fusion.4 = (bf16[1024,1,256]{2,0,1:T(8,128)(2,1)S(1)}, bf16[1024,1,256]{2,0,1:T(8,128)(2,1)S(1)}) fusion(s32[256]{0:T(256)S(1)} %iota_add_fusion.4), kind=kLoop, calls=%fused_computation.9.clone.1 | loop fusion | flops 2883584 | bytes 1049600 | tf_op jit(solution)/shard_map/convert
  176.2 4.6 %cosine_convert_fusion.4 = (bf16[1024,1,256]{2,0,1:T(8,128)(2,1)S(1)}, bf16[1024,1,256]{2,0,1:T(8,128)(2,1)S(1)}) fusion(s32[256]{0:T(256)S(1)} %iota_add_fusion.4), kind=kLoop, calls=%fused_computation.9.clone.1 | loop fusion | flops 2883584 | bytes 1049600 | tf_op jit(solution)/shard_map/convert
  192.4 23.0 %all_to_all.96 = f32[128,1,192]{2,1,0:T(1,128)S(1)} all-to-all(f32[128,1,192]{2,1,0:T(1,128)S(1)} %reshape.340), channel_id=1, replica_groups=mesh['blk'=128,'fld'=4] {'blk'}, dimensions={0} | all-to-all | bytes 196608 | tf_op jit(solution)/shard_map/all_to_all | solution.py:97
  219.5 7.3 %all-to-all-start.4 = ((f32[128,1,192]{2,1,0:T(1,128)}), f32[128,1,192]{2,1,0:T(1,128)S(1)}, u32[]{:S(2)}, u32[]{:S(2)}) async-start(f32[128,1,192]{2,1,0:T(1,128)} %reshape.342), calls=%async_computation.4 | async-start | bytes 262144 | tf_op jit(solution)/shard_map/all_to_all | solution.py:99
  228.4 15.7 %all-to-all-done.4 = f32[128,1,192]{2,1,0:T(1,128)S(1)} async-done(((f32[128,1,192]{2,1,0:T(1,128)}), f32[128,1,192]{2,1,0:T(1,128)S(1)}, u32[]{:S(2)}, u32[]{:S(2)}) %all-to-all-start.4) | async-done | bytes 98336 | tf_op jit(solution)/shard_map/all_to_all | solution.py:99
  245.2 7.3 %scatter_custom_fusion = f32[5120,32]{1,0:T(8,128)} fusion(s32[768]{0:T(1024)S(1)} %reshape.313, f32[]{:T(128)} %constant.124.clone.1, f32[32,768]{0,1:T(8,128)S(1)} %all_to_all.81), kind=kCustom, calls=%fused_computation.47 | custom fusion | flops 24576 | bytes 1048580 | tf_op jit(solution)/shard_map/scatter-add | solution.py:100
  252.5 4.8 %multiply_bitcast_fusion.5 = (f32[2,32,2560]{1,2,0:T(8,128)S(1)}, f32[2,32,2560]{1,2,0:T(8,128)S(1)}, f32[2,32,2560]{1,2,0:T(8,128)S(1)}, f32[2,32,2560]{1,2,0:T...) fusion(f32[32,2,2560]{0,2,1:T(8,128)} %bitcast.146, f32[32]{0:T(128)S(1)} %get-tuple-element.210, ...), kind=kLoop, calls=%fused_computation.41 | loop fusion | flops 983040 | bytes 4588288 | tf_op jit(solution)/shard_map/mul | solution.py:31
  257.2 5.6 %fusion.17 = bf16[2,32,2560]{1,2,0:T(8,128)(2,1)S(1)} fusion(f32[2,32,2560]{1,2,0:T(8,128)S(1)} %get-tuple-element.201, f32[2,32,2560]{1,2,0:T(8,128)S(1)} %get-tuple-element.202, f32[2,32,2560]{1,2,0:T(8,128)S(1)} %get-tuple-element.203, f32[32,2,2560]{0,2,1:T(8,128)S(1)} %bitcast.147, f32[2,32,2560]{1,2,0:T(8,128)S(1)} %get-tuple-element.204, ...), kind=kLoop, calls=%fused_computation.35 | loop fusion | flops 1310720 | bytes 4915328 | tf_op jit(solution)/shard_map/convert_element_type | solution.py:102
  264.0 84.7 %while.29 = (s32[]{:T(128)}, f32[2048,64]{0,1:T(8,128)}, bf16[64,2560]{1,0:T(8,128)(2,1)}, s32[]{:T(128)}, s32[]{:T(128)}, /*index=5*/s32[]{:T(128)}, s32[]{:T(128)}) while((s32[]{:T(128)}, f32[2048,64]{0,1:T(8,128)}, bf16[64,2560]{1,0:T(8,128)(2,1)}, s32[]{:T(128)}, s32[]{:T(128)}, /*index=5*/s32[]{:T(128)}, s32[]{:T(128)}) %tuple.89), condition=%wide.region_5.6_spmd.clone, body=%wide.region_4.5_spmd.clone.sunk | while | flops 70779144 | bytes 9472141 | solution.py:112
  351.5 26.9 %all_to_all.97 = bf16[128,2,512]{2,1,0:T(2,128)(2,1)S(1)} all-to-all(bf16[128,2,512]{2,1,0:T(2,128)(2,1)S(1)} %reshape.344), channel_id=1, replica_groups=mesh['blk'=128,'fld'=4] {'blk'}, dimensions={0} | all-to-all | bytes 524288 | tf_op jit(solution)/shard_map/all_to_all | solution.py:120
  379.8 12.7 %all_to_all.98 = bf16[1,8,256,2,1,32]{2,5,4,3,0,1:T(8,128)(2,1)S(1)} all-to-all(bf16[1,8,256,2,1,32]{2,5,4,3,0,1:T(8,128)(2,1)S(1)} %copy.96), channel_id=1, replica_groups=mesh['blk'=128,'fld'=4] {'fld'}, dimensions={1} | all-to-all | bytes 524288 | tf_op jit(solution)/shard_map/all_to_all | solution.py:119
  (195 shorter events, 170.6 us)
Async XLA Ops:
  0.0 27.6 %copy-start = (bf16[2,256,1280]{2,1,0:T(8,128)(2,1)S(1)}, bf16[2,256,1280]{2,1,0:T(8,128)(2,1)}, u32[]{:S(2)}) copy-start(bf16[2,256,1280]{2,1,0:T(8,128)(2,1)} %param.13) | copy-start | bytes 3932164
  4.6 38.9 %all-to-all-start = ((s32[1,128,6]{2,0,1:T(1,128)}), s32[1,128,6]{2,0,1:T(1,128)S(1)}, u32[]{:S(2)}, u32[]{:S(2)}) async-start(s32[1,128,6]{2,0,1:T(1,128)} %bitcast.9), calls=%async_computation | async-start | bytes 131072 | tf_op jit(solution)/shard_map/all_to_all | solution.py:92
  27.6 22.6 %copy-start.2 = (f32[1,7,32]{2,0,1:T(1,128)S(1)}, f32[1,7,32]{2,0,1:T(1,128)}, u32[]{:S(2)}) copy-start(f32[1,7,32]{2,0,1:T(1,128)} %param.14) | copy-start | bytes 2692
  43.5 29.2 %all-to-all-start.1 = ((bf16[128,2,512]{2,1,0:T(2,128)(2,1)}), bf16[128,2,512]{2,1,0:T(2,128)(2,1)S(1)}, u32[]{:S(2)}, u32[]{:S(2)}) async-start(bf16[128,2,512]{2,1,0:T(2,128)(2,1)} %reshape.338), calls=%async_computation.1 | async-start | bytes 524288 | tf_op jit(solution)/shard_map/all_to_all | solution.py:56
  75.2 12.5 %all-to-all-start.2 = ((bf16[128,2,2,2,4,32]{0,5,3,2,1,4:T(8,128)(2,1)}), bf16[128,2,2,2,4,32]{0,5,3,2,1,4:T(8,128)(2,1)S(1)}, u32[]{:S(2)}, u32[]{:S(2)}) async-start(bf16[128,2,2,2,4,32]{0,5,3,2,1,4:T(8,128)(2,1)} %copy.85), calls=%async_computation.2 | async-start | bytes 524288 | tf_op jit(solution)/shard_map/all_to_all | solution.py:55
  191.9 25.3 %copy-start.4 = (bf16[1,32,512]{2,1,0:T(8,128)(2,1)S(1)}, bf16[1,32,512]{2,1,0:T(8,128)(2,1)}, u32[]{:S(2)}) copy-start(bf16[1,32,512]{2,1,0:T(8,128)(2,1)} %param.15) | copy-start | bytes 98308
  192.0 25.7 %copy-start.3 = (f32[1,32,512]{2,1,0:T(8,128)S(1)}, f32[1,32,512]{2,1,0:T(8,128)}, u32[]{:S(2)}) copy-start(f32[1,32,512]{2,1,0:T(8,128)} %param.16) | copy-start | bytes 196612
  219.5 24.6 %all-to-all-start.4 = ((f32[128,1,192]{2,1,0:T(1,128)}), f32[128,1,192]{2,1,0:T(1,128)S(1)}, u32[]{:S(2)}, u32[]{:S(2)}) async-start(f32[128,1,192]{2,1,0:T(1,128)} %reshape.342), calls=%async_computation.4 | async-start | bytes 262144 | tf_op jit(solution)/shard_map/all_to_all | solution.py:99
  252.5 4.8 %copy-start.1 = (f32[5120,32]{1,0:T(8,128)S(1)}, f32[5120,32]{1,0:T(8,128)}, u32[]{:S(2)}) copy-start(f32[5120,32]{1,0:T(8,128)} %scatter_custom_fusion) | copy-start | bytes 1966084
where the time goes:
time: 396 us; the launch traced here: 394 us
  other arithmetic  116 us (29%)
  blocking collectives  62.6 us (16%)
  local copies, waits for them, and re-layouts  61.2 us (15%)
  waiting for transfers between devices  54.7 us (14%)
  matrix products  47 us (12%)
  starting transfers between devices  44.2 us (11%)
  loops' own time  7.17 us (2%)
    another operation x20, other arithmetic  90.9 us
    all_to_all x1, blocking collectives, on_device(): lax.all_to_all(wave, 'blk', split_axis=0, concat_axis=2, tiled=True)  26.9 us
    all_to_all x1, blocking collectives, on_device(): lax.all_to_all(found, 'blk', split_axis=1, concat_axis=1, tiled=True)  23 us
    all_to_all x1, starting transfers between devices, on_device(): lax.all_to_all(sent_spots.astype(jnp.int32), 'blk', split_axis=1, concat_...  23 us
    dot_general x10, matrix products, adjoint_block(): lax.dot_general(table, piece, (((1,), (1,)), ((), ())), preferred_element...  22.8 us
    all_to_all x1, waiting for transfers between devices, on_device(): lax.all_to_all(four, 'blk', split_axis=2, concat_axis=0, tiled=True)  22.3 us
    another operation x20, local copies, waits for them, and re-layouts, zonal_table(): both = jnp.stack([jnp.cos(angle), jnp.sin(angle)], axis=1)  21.6 us
    dot_general x10, matrix products, forward_block(): return jnp.dot(rows, table, preferred_element_type=jnp.float32)  18.8 us
  transfers between devices with their start and end apart: 4, of which 4 were waited for; matrix products, arithmetic and copies ran while one was open for 2% of the time, Pallas kernels for 0%

commit v1 on v0

v1 whole, which is shorter than its diff:
```python
import functools
import math

import jax
import jax.numpy as jnp
import numpy as np
from jax import lax
from jax.experimental import pallas as pl
from jax.experimental.pallas import tpu as pltpu
from jax.sharding import PartitionSpec as P

NLON = 2560
NY = 4
SLOT_ROWS = 4
MESH = pl.DeviceIdType.MESH
F32 = jnp.float32
BF16 = jnp.bfloat16


def power_series(f, terms):
    fit = np.polynomial.chebyshev.Chebyshev.interpolate(f, terms - 1, domain=[0.0, 0.25])
    return [float(c) for c in fit.convert(kind=np.polynomial.Polynomial).coef]


def cos_series():
    return power_series(lambda v: np.cos(2 * np.pi * np.sqrt(v)), 7)


def sin_series():
    return power_series(lambda v: 2 * np.pi * np.sinc(2 * np.sqrt(v)), 7)


def horner(coefs, v):
    total = jnp.full_like(v, coefs[-1])
    for c in coefs[-2::-1]:
        total = total * v + c
    return total


def cos_sin(turns, whole):
    rest = turns - jnp.round(turns * (1.0 / whole)) * whole
    u = rest * (1.0 / whole)
    v = u * u
    return horner(cos_series(), v), u * horner(sin_series(), v)


def dot(a, b, dims=(1, 0), precision=None):
    return lax.dot_general(
        a, b, (((dims[0],), (dims[1],)), ((), ())), precision=precision, preferred_element_type=F32
    )


def iota(shape, axis):
    return lax.broadcasted_iota(jnp.int32, shape, axis)


def kernel(
    nblk, nfld, ny, leg_hbm, coef_hbm, vcoef_ref, val_ref, wgt_ref, dest_ref, spot_ref, count_ref, wave_ref,
    leg, coef, rows_f, tmp_a, tmp_o, tmp_p, send_a, recv_a, send_b, recv_b, send_oa, recv_oa, send_ob, recv_ob,
    send_c, recv_c, send_d, recv_d, spot_col, spot_row, tcos, tsin, ucos, usin,
    load_sem, sa_s, sa_r, sb_s, sb_r, oa_s, oa_r, ob_s, ob_r, sc_s, sc_r, sd_s, sd_r,
):
    nxz = nblk // ny
    nz = nxz // 2
    group = ny * nfld
    waves, lat = leg.shape[0], leg.shape[1]
    members = group * waves
    total_m = nxz * members
    levels = vcoef_ref.shape[1]
    band = vcoef_ref.shape[0]
    half = (band - 1) // 2
    lanes = 4 * levels
    obs_dev = dest_ref.shape[1]
    orows = nblk * SLOT_ROWS

    b = lax.axis_index("blk")
    f = lax.axis_index("fld")
    y = lax.rem(b, ny)
    xz = lax.div(b, ny)
    member = y * nfld + f

    def xz_partner(i):
        flip = lax.rem(i, 2)
        t = lax.div(i, 2)
        step = lax.div(t + 1, 2)
        move = jnp.where(lax.rem(t, 2) == 1, step, nz - step)
        x_hi = lax.rem(lax.div(xz, nz) + flip, 2)
        z = lax.rem(lax.rem(xz, nz) + move, nz)
        return x_hi * nz + z

    def group_partner(i):
        return lax.rem(member + i, group)

    def y_partner(i):
        return lax.rem(y + i, ny)

    def group_device(mem):
        return (xz * ny + lax.div(mem, nfld), lax.rem(mem, nfld))

    def xz_device(other):
        return (other * ny + y, f)

    def y_device(other):
        return (xz * ny + other, f)

    def copy_of(src, dst, where_from, where_to, send_sem, recv_sem, device):
        return pltpu.make_async_remote_copy(
            src_ref=src.at[where_from], dst_ref=dst.at[where_to], send_sem=send_sem.at[where_from],
            recv_sem=recv_sem.at[where_to], device_id=device, device_id_type=MESH,
        )

    def start_all(count, partner, device, src, dst, mine, send_sem, recv_sem):
        def step(k, carry):
            other = partner(count - 1 - k)
            copy_of(src, dst, other, mine, send_sem, recv_sem, device(other)).start()
            return carry

        lax.fori_loop(0, count - 1, step, 0)
        dst[mine] = src[mine]

    def recv_all(count, partner, device, src, dst, send_sem, recv_sem):
        def step(k, carry):
            other = partner(count - 1 - k)
            copy_of(src, dst, other, other, send_sem, recv_sem, device(other)).wait_recv()
            return carry

        lax.fori_loop(0, count - 1, step, 0)

    def send_done(count, partner, device, src, dst, send_sem, recv_sem):
        def step(k, carry):
            other = partner(count - 1 - k)
            copy_of(src, dst, other, other, send_sem, recv_sem, device(other)).wait_send()
            return carry

        lax.fori_loop(0, count - 1, step, 0)

    in_group = (group, group_partner, group_device)
    in_xz = (nxz, xz_partner, xz_device)
    in_y = (ny, y_partner, y_device)

    load_leg = pltpu.make_async_copy(leg_hbm, leg, load_sem.at[0])
    load_coef = pltpu.make_async_copy(coef_hbm, coef, load_sem.at[1])
    load_coef.start()
    load_leg.start()
    barrier = pltpu.get_barrier_semaphore()

    def greet(count, partner, device):
        def step(i, carry):
            pl.semaphore_signal(barrier, inc=1, device_id=device(partner(i)), device_id_type=MESH)
            return carry

        lax.fori_loop(1, count, step, 0)

    greet(*in_group)
    greet(*in_xz)

    dest = dest_ref[...]
    spot = spot_ref[...]
    order = iota((1, obs_dev), 1)
    live = order < count_ref[0]
    onehot = (iota((nblk, obs_dev), 0) == dest).astype(F32)
    earlier = (iota((obs_dev, obs_dev), 0) < iota((obs_dev, obs_dev), 1)).astype(BF16)
    before = dot(onehot.astype(BF16), earlier)
    rank = jnp.sum(before * onehot, axis=0, keepdims=True).astype(jnp.int32)
    place = (lax.rem(dest, ny) * nxz + lax.div(dest, ny)) * SLOT_ROWS
    place = jnp.where(live, place, -SLOT_ROWS)
    pair = place + lax.div(rank, 2)
    second = lax.rem(rank, 2) == 1
    row = iota((orows, obs_dev), 0)
    pick_first = (row == jnp.where(second, -1, pair)).astype(BF16)
    pick_second = (row == jnp.where(second, pair, -1)).astype(BF16)
    pick_place = (row == place + SLOT_ROWS - 1).astype(BF16)
    data = jnp.concatenate([val_ref[...].astype(F32), wgt_ref[...]], axis=0).astype(BF16)
    lane_q = iota((lanes // 2, obs_dev), 0)
    high = lax.div(spot, 32)
    low = spot - high * 32
    spots = jnp.where(lane_q == rank, high, jnp.where(lane_q == rank + 8, low, 0)).astype(F32).astype(BF16)
    none = jnp.zeros((lanes // 2, obs_dev), BF16)
    packed = dot(pick_first, jnp.concatenate([data, none], axis=0), (1, 1))
    packed = packed + dot(pick_second, jnp.concatenate([none, data], axis=0), (1, 1))
    packed = packed + dot(pick_place, jnp.concatenate([spots, none], axis=0), (1, 1))
    send_oa[...] = packed.astype(BF16).reshape(send_oa.shape)

    def greet_wait():
        pl.semaphore_wait(barrier, group - 1 + nxz - 1)

    load_coef.wait()
    load_leg.wait()
    for w in range(waves):
        result = dot(leg[w], coef[w])
        for r in range(2):
            rows_f[pl.ds((r * waves + w) * lat, lat), :] = result[:, r * lanes : (r + 1) * lanes]
    greet_wait()
    start_all(*in_y, send_oa, recv_oa, y, oa_s, oa_r)

    chunk = lax.div(iota((nxz, lanes), 1), levels)

    def pack(step, carry):
        w, yy = lax.div(step, ny), lax.rem(step, ny)
        parts = []
        for r in range(2):
            for j in range(2):
                parts.append(rows_f[pl.ds((r * waves + w) * lat + 2 * yy + j, nxz, stride=2 * ny), :])
        for ff in range(nfld):
            out = parts[0] if ff == 0 else pltpu.roll(parts[0], (0 - ff) % 4 * levels, 1)
            for k in range(1, 4):
                moved = parts[k] if ff == k else pltpu.roll(parts[k], (k - ff) % 4 * levels, 1)
                out = jnp.where(chunk == k, moved, out)
            send_a[yy * nfld + ff, pl.ds(pl.multiple_of(w * nxz, nxz), nxz), :] = out.astype(BF16)
        return carry

    lax.fori_loop(0, waves * ny, pack, 0)
    start_all(*in_group, send_a, recv_a, member, sa_s, sa_r)

    recv_all(*in_y, send_oa, recv_oa, oa_s, oa_r)
    tmp_o[...] = recv_oa[...].astype(F32).reshape(tmp_o.shape)
    for yy in range(ny):
        for k in range(SLOT_ROWS):
            rows = tmp_o[pl.ds(yy * nxz * SLOT_ROWS + k, nxz, stride=SLOT_ROWS), :]
            tmp_p[pl.ds(yy * SLOT_ROWS + k, nxz, stride=ny * SLOT_ROWS), :] = rows
    send_ob[...] = tmp_p[...].astype(BF16).reshape(send_ob.shape)
    start_all(*in_xz, send_ob, recv_ob, xz, ob_s, ob_r)

    def swap(src, dst, outer, inner):
        tmp_a[...] = src[...].astype(F32).reshape(tmp_a.shape)
        for i in range(inner):
            rows = tmp_a[pl.ds(i, outer, stride=inner), :]
            per = dst.shape[1] // outer
            dst[i // per, pl.ds(i % per * outer, outer), :] = rows.astype(BF16)

    recv_all(*in_group, send_a, recv_a, sa_s, sa_r)
    swap(recv_a, send_b, members, nxz)
    start_all(*in_xz, send_b, recv_b, xz, sb_s, sb_r)

    recv_all(*in_xz, send_ob, recv_ob, ob_s, ob_r)
    got = recv_ob[...].reshape(orows, lanes)
    in_row = lax.rem(iota((orows, orows), 0), SLOT_ROWS)
    places = iota((orows, orows), 0) - in_row + (SLOT_ROWS - 1)
    spread = dot((iota((orows, orows), 1) == places).astype(BF16), got)
    lane = iota((orows, lanes), 1)
    k_row = lax.rem(iota((orows, lanes), 0), SLOT_ROWS)
    ones = jnp.ones((lanes, lanes), BF16)
    base = min(lanes, total_m)
    for h in range(2):
        q = 2 * k_row + h
        mine = jnp.where(lane == q, spread * 32.0, jnp.where(lane == q + 8, spread, 0.0)).astype(BF16)
        spot_col[h] = dot(mine, ones)
        spot_row[h] = dot(ones, mine, (1, 1))

    def longitude(s):
        return jnp.where(s >= NLON, s - NLON, s)

    def turn(c, s, c1, s1):
        return c * c1 - s * s1, s * c1 + c * s1

    tile = min(64, orows)
    for h in range(2):
        def along_m(i, carry):
            here = pl.ds(pl.multiple_of(i * tile, tile), tile)
            lon = longitude(spot_col[h, here, pl.ds(0, base)])
            c, s = cos_sin(lon * iota((tile, base), 1).astype(F32), NLON)
            c1, s1 = cos_sin(lon * float(base), NLON)
            for q in range(total_m // base):
                tcos[h, here, pl.ds(q * base, base)] = c.astype(BF16)
                tsin[h, here, pl.ds(q * base, base)] = s.astype(BF16)
                c, s = turn(c, s, c1, s1)
            return carry

        lax.fori_loop(0, orows // tile, along_m, 0)

    deep = min(64, total_m)
    wide = min(128, orows)
    for h in range(2):
        def along_o(i, carry):
            here = pl.ds(pl.multiple_of(i * wide, wide), wide)
            lon = longitude(spot_row[h, pl.ds(0, deep), here])
            c, s = cos_sin(lon * iota((deep, wide), 0).astype(F32), NLON)
            c1, s1 = cos_sin(lon * float(deep), NLON)
            for q in range(total_m // deep):
                ucos[h, pl.ds(q * deep, deep), here] = c.astype(BF16)
                usin[h, pl.ds(q * deep, deep), here] = s.astype(BF16)
                c, s = turn(c, s, c1, s1)
            return carry

        lax.fori_loop(0, orows // wide, along_o, 0)

    scale = 1.0 / math.sqrt(total_m)
    vc = jnp.concatenate([vcoef_ref[...]] * 4, axis=1) * scale
    lev_row = lax.rem(iota((lanes, lanes), 0), levels)
    lev_col = lax.rem(iota((lanes, lanes), 1), levels)
    up = jnp.zeros((lanes, lanes), F32)
    for k in range(band):
        up = up + jnp.where(lev_row == lev_col + (k - half), vc[k : k + 1, :], 0.0)
    ups, downs = [], []
    for h in range(2):
        in_half = lax.div(iota((lanes, lanes), 1), levels) == 2 * h
        first = lax.div(iota((lanes, lanes), 0), levels) < 2
        ups.append(jnp.where(in_half & first, up, 0.0))
        downs.append(jnp.where(in_half, up, 0.0))
    exact = lax.Precision.HIGHEST
    chunk_o = lax.div(lane, levels)
    got32 = got.astype(F32)
    weight = pltpu.roll(got32, lanes - levels, 1)
    weight = jnp.where(lax.rem(chunk_o, 2) == 0, weight, 0.0)

    recv_all(*in_xz, send_b, recv_b, sb_s, sb_r)
    four = recv_b[...].reshape(total_m, lanes)
    model = jnp.zeros((orows, lanes), F32)
    at_lat = []
    for h in range(2):
        at_lat.append(lax.rem(chunk_o, 2) == (spot_col[h] >= NLON).astype(jnp.int32))
        grid = dot(tcos[h], four) + pltpu.roll(dot(tsin[h], four), lanes // 2, 1)
        grid = jnp.where(at_lat[h] & (chunk_o < 2), grid, 0.0)
        model = model + dot(grid, ups[h], precision=exact)
    weighted = weight * (model - got32)
    wave = jnp.zeros((total_m, lanes), F32)
    for h in range(2):
        back = dot(weighted, downs[h], (1, 1), precision=exact)
        back = jnp.where(at_lat[h], back, 0.0)
        wave = wave + dot(ucos[h], jnp.where(chunk_o < 2, back, 0.0).astype(BF16))
        wave = wave + dot(usin[h], jnp.where(chunk_o < 2, 0.0, back).astype(BF16))
    send_c[...] = wave.astype(BF16).reshape(send_c.shape)
    start_all(*in_xz, send_c, recv_c, xz, sc_s, sc_r)
    recv_all(*in_xz, send_c, recv_c, sc_s, sc_r)
    swap(recv_c, send_d, nxz, members)
    start_all(*in_group, send_d, recv_d, member, sd_s, sd_r)
    recv_all(*in_group, send_d, recv_d, sd_s, sd_r)

    def unpack(step, carry):
        w, yy = lax.div(step, ny), lax.rem(step, ny)
        parts = [
            recv_d[yy * nfld + ff, pl.ds(pl.multiple_of(w * nxz, nxz), nxz), :].astype(F32)
            for ff in range(nfld)
        ]
        for r in range(2):
            for j in range(2):
                k = 2 * r + j
                out = parts[0] if k == 0 else pltpu.roll(parts[0], (0 - k) % 4 * levels, 1)
                for ff in range(1, nfld):
                    moved = parts[ff] if ff == k else pltpu.roll(parts[ff], (ff - k) % 4 * levels, 1)
                    out = jnp.where(chunk == ff, moved, out)
                rows_f[pl.ds((r * waves + w) * lat + 2 * yy + j, nxz, stride=2 * ny), :] = out
        return carry

    lax.fori_loop(0, waves * ny, unpack, 0)
    for w in range(waves):
        for r in range(2):
            rows = rows_f[pl.ds((r * waves + w) * lat, lat), :]
            wave_ref[w, :, pl.ds(r * lanes, lanes)] = rows.astype(BF16)

    for sent in (
        (*in_y, send_oa, recv_oa, oa_s, oa_r),
        (*in_group, send_a, recv_a, sa_s, sa_r),
        (*in_xz, send_ob, recv_ob, ob_s, ob_r),
        (*in_xz, send_b, recv_b, sb_s, sb_r),
        (*in_xz, send_c, recv_c, sc_s, sc_r),
        (*in_group, send_d, recv_d, sd_s, sd_r),
    ):
        send_done(*sent)


def on_device(coef, leg, vcoef, obs_value, obs_weight, obs_dest, obs_spot, obs_count, ny=NY):
    nblk = lax.axis_size("blk")
    nfld = lax.axis_size("fld")
    waves, lat, nn = leg.shape
    width = coef.shape[2]
    levels = vcoef.shape[2]
    lanes = 4 * levels
    nxz = nblk // ny
    group = ny * nfld
    members = group * waves
    total_m = nxz * members
    orows = nblk * SLOT_ROWS
    obs_dev = obs_spot.shape[0]

    def buffer(*shape):
        return pltpu.VMEM(shape, BF16)

    vmem = pl.BlockSpec(memory_space=pltpu.VMEM)
    scratch = [
        buffer(waves, lat, nn), buffer(waves, nn, width), pltpu.VMEM((2 * waves * lat, lanes), F32),
        pltpu.VMEM((total_m, lanes), F32), pltpu.VMEM((orows, lanes), F32), pltpu.VMEM((orows, lanes), F32),
        buffer(group, waves * nxz, lanes), buffer(group, waves * nxz, lanes),
        buffer(nxz, members, lanes), buffer(nxz, members, lanes),
        buffer(ny, nxz * SLOT_ROWS, lanes), buffer(ny, nxz * SLOT_ROWS, lanes),
        buffer(nxz, ny * SLOT_ROWS, lanes), buffer(nxz, ny * SLOT_ROWS, lanes),
        buffer(nxz, members, lanes), buffer(nxz, members, lanes),
        buffer(group, waves * nxz, lanes), buffer(group, waves * nxz, lanes),
        pltpu.VMEM((2, orows, lanes), F32), pltpu.VMEM((2, lanes, orows), F32),
        buffer(2, orows, total_m), buffer(2, orows, total_m),
        buffer(2, total_m, orows), buffer(2, total_m, orows),
        pltpu.SemaphoreType.DMA((2,)),
    ]
    for count in (group, nxz, ny, nxz, nxz, group):
        scratch += [pltpu.SemaphoreType.DMA((count,)), pltpu.SemaphoreType.DMA((count,))]
    wave = pl.pallas_call(
        functools.partial(kernel, nblk, nfld, ny),
        out_shape=jax.ShapeDtypeStruct((waves, lat, width), BF16),
        in_specs=[
            pl.BlockSpec(memory_space=pl.ANY), pl.BlockSpec(memory_space=pl.ANY), vmem, vmem, vmem, vmem, vmem,
            pl.BlockSpec(memory_space=pltpu.SMEM),
        ],
        out_specs=vmem,
        scratch_shapes=scratch,
        compiler_params=pltpu.CompilerParams(
            collective_id=0, has_side_effects=True, vmem_limit_bytes=48 * 1024 * 1024
        ),
    )(leg, coef, vcoef[0], obs_value[0], obs_weight[0], obs_dest.reshape(1, obs_dev), obs_spot.reshape(1, obs_dev), obs_count)
    return jnp.einsum("mjn,mjc->mnc", leg, wave, preferred_element_type=F32).astype(BF16)


def solution(mesh):
    in_specs = (
        P(("blk", "fld"), None, None),
        P(("blk", "fld"), None, None),
        P("fld", None, None),
        P("fld", None, "blk"),
        P("fld", None, "blk"),
        P("blk", None),
        P("blk"),
        P("blk"),
    )
    out_specs = P(("blk", "fld"), None, None)
    return jax.shard_map(
        on_device, mesh=mesh, in_specs=in_specs, out_specs=out_specs, check_vma=False
    )
```

time: 396 us -> 82.1 us (0.21)
  other arithmetic: 116 us -> 0 us
  Pallas kernels: 0 us -> 72.8 us
  blocking collectives: 62.6 us -> 0 us
  waiting for transfers between devices: 54.7 us -> 0 us
  local copies, waits for them, and re-layouts: 61.2 us -> 7.72 us
  matrix products: 47 us -> 0.56 us
  starting transfers between devices: 44.2 us -> 0 us
  loops' own time: 7.17 us -> 0 us
    another operation x40 -> x0, other arithmetic: 92.8 us -> none
    pallas_call x0 -> x1, Pallas kernels: none -> 72.8 us  [on_device(): pl.pallas_call(functools.partial(kernel, nblk, nfld, ny), out_shape=jax.S...]
    all_to_all x3 -> x0, blocking collectives: 62.6 us -> none  [the longest x1 26.9 us: on_device(): lax.all_to_all(wave, 'blk', split_axis=0, concat_axis=2, tiled=True)]
    all_to_all x4 -> x0, waiting for transfers between devices: 54.7 us -> none  [the longest x1 22.3 us: on_device(): lax.all_to_all(four, 'blk', split_axis=2, concat_axis=0, tiled=True)]
    dot_general x26 -> x1, matrix products: 47 us -> 0.56 us  [on_device(): jnp.einsum('mjn,mjc->mnc', leg, wave, preferred_element_type=F32)]
    all_to_all x4 -> x0, starting transfers between devices: 44.2 us -> none  [the longest x1 23 us: on_device(): lax.all_to_all(sent_spots.astype(jnp.int32), 'blk', split_axis=1, concat_...]
    another operation x22 -> x0, local copies, waits for them, and re-layouts: 21.9 us -> none  [the longest x20 21.6 us: zonal_table(): both = jnp.stack([jnp.cos(angle), jnp.sin(angle)], axis=1)]
    convert_element_type x23 -> x1, local copies, waits for them, and re-layouts: 11.7 us -> 1.44 us  [on_device(): jnp.einsum('mjn,mjc->mnc', leg, wave, preferred_element_type=F32)]
  transfers between devices with their start and end apart: 4 -> 0, of which waited for: 4 -> 0; matrix products, arithmetic and copies ran while one was open for 2% -> 0% of each run, Pallas kernels for 0% -> 0%
where the time goes in v1:
time: 82.1 us; the launch traced here: 81.7 us
  Pallas kernels  72.8 us (89%)
  local copies, waits for them, and re-layouts  7.72 us (9%)
    pallas_call x1, Pallas kernels, on_device(): pl.pallas_call(functools.partial(kernel, nblk, nfld, ny), out_shape=jax.S...  72.8 us
    unnamed x13, local copies, waits for them, and re-layouts  6.28 us

profile of v1, /device:TPU:1, one launch (start us, length us, event | category | flops | bytes accessed | tf_op | source)
XLA Modules:
  0.0 81.7 jit_solution(15414699756766365815)
XLA Ops:
  0.7 0.7 copy.14
  1.3 0.0 copy-start
  1.3 1.3 %copy-done = bf16[2,256,1280]{2,1,0:T(8,128)(2,1)S(1)} copy-done((bf16[2,256,1280]{2,1,0:T(8,128)(2,1)S(1)}, bf16[2,256,1280]{2,1,0:T(8,128)(2,1)}, u32[]{:S(2)}) %copy-start) | copy-done | bytes 1310744
  2.7 0.0 copy-start.1
  2.7 1.3 %copy-done.1 = bf16[2,1280,256]{2,1,0:T(8,128)(2,1)S(1)} copy-done((bf16[2,1280,256]{2,1,0:T(8,128)(2,1)S(1)}, bf16[2,1280,256]{2,1,0:T(8,128)(2,1)}, u32[]{:S(2)}) %copy-start.1) | copy-done | bytes 1310744
  4.0 0.0 copy-start.2
  4.0 0.8 %copy-done.2 = f32[1,32,512]{2,1,0:T(8,128)S(1)} copy-done((f32[1,32,512]{2,1,0:T(8,128)S(1)}, f32[1,32,512]{2,1,0:T(8,128)}, u32[]{:S(2)}) %copy-start.2) | copy-done | bytes 65560
  4.8 0.0 copy-start.3
  4.8 0.8 copy-done.3
  5.6 0.0 copy-start.4
  5.6 0.7 copy-done.4
  6.3 0.0 copy-start.5
  6.3 0.7 copy-done.5
  6.9 72.8 %shard_map.82 = bf16[2,256,256]{2,1,0:T(8,128)(2,1)S(1)} custom-call(bf16[2,256,1280]{2,1,0:T(8,128)(2,1)S(1)} %copy-done, bf16[2,1280,256]{2,1,0:T(8,128)(2,1)S(1)} %copy-done.1, f32[7,32]{1,0:T(8,128)S(1)} %bitcast.13, bf16[32,512]{1,0:T(8,128)(2,1)S(1)} %bitcast.12, f32[32,512]{1,0:T(8,128)S(1)} %bitcast.11, s32[1,512]{1,0:T(1,128)S(1)} %bitcast.14, ...), custom_call_target="tpu_custom_call" | custom-call | tf_op jit(solution)/shard_map/pallas_call | solution.py:396
  79.7 0.6 fusion
  80.3 1.4 %copy.10 = bf16[2,1280,256]{2,1,0:T(8,128)(2,1)} copy(bf16[2,1280,256]{1,2,0:T(8,128)(2,1)S(1)} %fusion) | data formatting | bytes 2621440 | tf_op jit(solution)/shard_map/convert_element_type | solution.py:409
Async XLA Ops:
  1.3 1.3 %copy-start = (bf16[2,256,1280]{2,1,0:T(8,128)(2,1)S(1)}, bf16[2,256,1280]{2,1,0:T(8,128)(2,1)}, u32[]{:S(2)}) copy-start(bf16[2,256,1280]{2,1,0:T(8,128)(2,1)} %leg_hbm.1) | copy-start | bytes 3932164
  2.7 1.3 %copy-start.1 = (bf16[2,1280,256]{2,1,0:T(8,128)(2,1)S(1)}, bf16[2,1280,256]{2,1,0:T(8,128)(2,1)}, u32[]{:S(2)}) copy-start(bf16[2,1280,256]{2,1,0:T(8,128)(2,1)} %coef_hbm.1) | copy-start | bytes 3932164
  4.0 0.8 %copy-start.2 = (f32[1,32,512]{2,1,0:T(8,128)S(1)}, f32[1,32,512]{2,1,0:T(8,128)}, u32[]{:S(2)}) copy-start(f32[1,32,512]{2,1,0:T(8,128)} %param.12) | copy-start | bytes 196612
  4.8 0.8 copy-start.3
  5.6 0.7 copy-start.4
  6.3 0.7 copy-start.5

commit v2 on v1

v2 whole, which is shorter than its diff:
```python
import functools
import math

import jax
import jax.numpy as jnp
import numpy as np
from jax import lax
from jax.experimental import pallas as pl
from jax.experimental.pallas import tpu as pltpu
from jax.sharding import PartitionSpec as P

NLON = 2560
NY = 4
SLOT_ROWS = 4
MESH = pl.DeviceIdType.MESH
F32 = jnp.float32
BF16 = jnp.bfloat16


def power_series(f, terms):
    fit = np.polynomial.chebyshev.Chebyshev.interpolate(f, terms - 1, domain=[0.0, 0.25])
    return [float(c) for c in fit.convert(kind=np.polynomial.Polynomial).coef]


def cos_series():
    return power_series(lambda v: np.cos(2 * np.pi * np.sqrt(v)), 7)


def sin_series():
    return power_series(lambda v: 2 * np.pi * np.sinc(2 * np.sqrt(v)), 7)


def horner(coefs, v):
    total = jnp.full_like(v, coefs[-1])
    for c in coefs[-2::-1]:
        total = total * v + c
    return total


def cos_sin(turns, whole):
    rest = turns - jnp.round(turns * (1.0 / whole)) * whole
    u = rest * (1.0 / whole)
    v = u * u
    return horner(cos_series(), v), u * horner(sin_series(), v)


def dot(a, b, dims=(1, 0), precision=None):
    return lax.dot_general(
        a, b, (((dims[0],), (dims[1],)), ((), ())), precision=precision, preferred_element_type=F32
    )


def iota(shape, axis):
    return lax.broadcasted_iota(jnp.int32, shape, axis)


def kernel(
    nblk, nfld, ny, leg_hbm, coef_hbm, vcoef_hbm, val_hbm, wgt_hbm, dest_hbm, spot_hbm, count_ref, wave_hbm, turned_hbm,
    wave_ref, turned_ref, leg, coef, vcoef_ref, val_ref, wgt_ref, dest_ref, spot_ref, rows_f, tmp_o, send_a, recv_a, send_b, recv_b, send_oa, recv_oa, send_ob, recv_ob,
    send_c, recv_c, send_d, recv_d, spot_col, spot_row, table, flipped,
    load_sem, store_sem, sa_s, sa_r, sb_s, sb_r, oa_s, oa_r, ob_s, ob_r, sc_s, sc_r, sd_s, sd_r,
):
    nxz = nblk // ny
    nz = nxz // 2
    group = ny * nfld
    waves, lat = leg.shape[0], leg.shape[1]
    part_m = nxz * group
    total_m = waves * part_m
    levels = vcoef_ref.shape[2]
    band = vcoef_ref.shape[0]
    half = (band - 1) // 2
    lanes = 4 * levels
    obs_dev = dest_ref.shape[1]
    orows = nblk * SLOT_ROWS

    b = lax.axis_index("blk")
    f = lax.axis_index("fld")
    y = lax.rem(b, ny)
    xz = lax.div(b, ny)
    member = y * nfld + f

    def xz_partner(i):
        flip = lax.rem(i, 2)
        t = lax.div(i, 2)
        step = lax.div(t + 1, 2)
        move = jnp.where(lax.rem(t, 2) == 1, step, nz - step)
        x_hi = lax.rem(lax.div(xz, nz) + flip, 2)
        z = lax.rem(lax.rem(xz, nz) + move, nz)
        return x_hi * nz + z

    def group_partner(i):
        return lax.rem(member + i, group)

    def y_partner(i):
        return lax.rem(y + i, ny)

    def group_device(mem):
        return (xz * ny + lax.div(mem, nfld), lax.rem(mem, nfld))

    def xz_device(other):
        return (other * ny + y, f)

    def y_device(other):
        return (xz * ny + other, f)

    def start_all(part, count, partner, device, mine, src, dst, send_sem, recv_sem):
        def step(k, carry):
            other = partner(count - 1 - k)
            pltpu.make_async_remote_copy(
                src_ref=src.at[part, other], dst_ref=dst.at[part, mine], send_sem=send_sem.at[part],
                recv_sem=recv_sem.at[part], device_id=device(other), device_id_type=MESH,
            ).start()
            return carry

        lax.fori_loop(0, count - 1, step, 0)
        dst[part, mine] = src[part, mine]

    def whole(part, count, partner, device, mine, src, dst, send_sem, recv_sem):
        others = pl.ds(0, count - 1)
        return pltpu.make_async_remote_copy(
            src_ref=src.at[part, others], dst_ref=dst.at[part, others], send_sem=send_sem.at[part],
            recv_sem=recv_sem.at[part], device_id=device(partner(1)), device_id_type=MESH,
        )

    def recv_all(part, *stage):
        whole(part, *stage).wait_recv()

    def send_done(part, *stage):
        whole(part, *stage).wait_send()

    in_group = (group, group_partner, group_device, member)
    in_xz = (nxz, xz_partner, xz_device, xz)
    in_y = (ny, y_partner, y_device, y)
    stage_a = (*in_group, send_a, recv_a, sa_s, sa_r)
    stage_b = (*in_xz, send_b, recv_b, sb_s, sb_r)
    stage_c = (*in_xz, send_c, recv_c, sc_s, sc_r)
    stage_d = (*in_group, send_d, recv_d, sd_s, sd_r)
    obs_xz = (*in_xz, send_ob, recv_ob, ob_s, ob_r)
    obs_y = (*in_y, send_oa, recv_oa, oa_s, oa_r)

    loads = [
        pltpu.make_async_copy(src, dst, load_sem.at[i])
        for i, (src, dst) in enumerate(
            (
                (dest_hbm, dest_ref), (spot_hbm, spot_ref), (val_hbm, val_ref), (wgt_hbm, wgt_ref),
                (vcoef_hbm, vcoef_ref), (coef_hbm, coef), (leg_hbm, leg),
            )
        )
    ]
    for load in loads:
        load.start()
    barrier = pltpu.get_barrier_semaphore()

    def greet(count, partner, device, mine):
        def step(i, carry):
            pl.semaphore_signal(barrier, inc=1, device_id=device(partner(i)), device_id_type=MESH)
            return carry

        lax.fori_loop(1, count, step, 0)

    greet(*in_group)
    greet(*in_xz)

    for load in loads[:5]:
        load.wait()

    dest = dest_ref[...]
    spot = spot_ref[...]
    live = iota((1, obs_dev), 1) < count_ref[0]
    place = jnp.where(live, lax.rem(dest, ny) * nxz + lax.div(dest, ny), -1)
    onehot = (iota((nblk, obs_dev), 0) == place).astype(BF16)
    part = min(128, obs_dev)
    upto = iota((part, 2 * part), 0) < iota((part, 2 * part), 1)
    ranks = []
    carry = jnp.zeros((nblk, part), F32)
    for i in range(obs_dev // part):
        piece = onehot[:, i * part : (i + 1) * part]
        counted = dot(piece, upto.astype(BF16))
        ranks.append(jnp.sum((counted[:, :part] + carry) * piece.astype(F32), axis=0, keepdims=True))
        carry = carry + counted[:, part:]
    rank = jnp.concatenate(ranks, axis=1).astype(jnp.int32)
    data = jnp.concatenate([val_ref[...].astype(F32), wgt_ref[...]], axis=0)
    lane_q = iota((lanes, obs_dev), 0)
    high = lax.div(spot, 32)
    low = spot - high * 32
    spots = jnp.where(lane_q == rank, high, jnp.where(lane_q == rank + 8, low, 0)).astype(F32)
    for k in range(SLOT_ROWS):
        rows = spots
        if k < SLOT_ROWS - 1:
            rows = [jnp.where(rank == 2 * k + h, data, 0.0) for h in range(2)]
            rows = jnp.concatenate(rows, axis=0)
        packed = dot(onehot, rows.astype(BF16), (1, 1))
        for yy in range(ny):
            tmp_o[pl.ds(yy * SLOT_ROWS + k, nxz, stride=ny * SLOT_ROWS), :] = packed[yy * nxz : (yy + 1) * nxz]
    send_ob[...] = tmp_o[...].astype(BF16).reshape(send_ob.shape)

    chunk = lax.div(iota((nxz, lanes), 1), levels)

    def legendre(w):
        result = dot(leg[w], coef[w])
        for r in range(2):
            rows_f[pl.ds((r * waves + w) * lat, lat), :] = result[:, r * lanes : (r + 1) * lanes]
        for yy in range(ny):
            parts = [
                rows_f[pl.ds((r * waves + w) * lat + 2 * yy + j, nxz, stride=2 * ny), :]
                for r in range(2)
                for j in range(2)
            ]
            for ff in range(nfld):
                out = parts[0] if ff == 0 else pltpu.roll(parts[0], (0 - ff) % 4 * levels, 1)
                for k in range(1, 4):
                    moved = parts[k] if ff == k else pltpu.roll(parts[k], (k - ff) % 4 * levels, 1)
                    out = jnp.where(chunk == k, moved, out)
                send_a[w, yy * nfld + ff] = out.astype(BF16)

    def swap(part, src, dst, outer, inner):
        tmp_o[...] = src[part].astype(F32).reshape(tmp_o.shape)
        per = dst.shape[2] // outer
        for i in range(inner):
            rows = tmp_o[pl.ds(i, outer, stride=inner), :]
            dst[part, i // per, pl.ds(i % per * outer, outer), :] = rows.astype(BF16)

    for load in loads[5:]:
        load.wait()
    legendre(0)
    pl.semaphore_wait(barrier, group - 1 + nxz - 1)
    start_all(0, *stage_a)
    start_all(0, *obs_xz)
    for w in range(1, waves):
        legendre(w)
        start_all(w, *stage_a)

    for w in range(waves):
        recv_all(w, *stage_a)
        swap(w, recv_a, send_b, group, nxz)
        start_all(w, *stage_b)

    recv_all(0, *obs_xz)
    swap(0, recv_ob, send_oa, nxz, ny * SLOT_ROWS)
    start_all(0, *obs_y)
    recv_all(0, *obs_y)

    got = recv_oa[...].reshape(orows, lanes)
    spread = [recv_oa[0, yy, pl.ds((SLOT_ROWS - 1) * nxz, nxz), :] for yy in range(ny) for k in range(SLOT_ROWS)]
    spread = jnp.concatenate(spread, axis=0).astype(F32)
    lane = iota((orows, lanes), 1)
    k_row = lax.rem(lax.div(iota((orows, lanes), 0), nxz), SLOT_ROWS)
    ones = jnp.ones((lanes, lanes), BF16)
    for h in range(2):
        q = 2 * k_row + h
        mine = jnp.where(lane == q, spread * 32.0, jnp.where(lane == q + 8, spread, 0.0)).astype(BF16)
        spot_col[h] = dot(mine, ones)
        spot_row[h] = dot(ones, mine, (1, 1))

    def longitude(s):
        return jnp.where(s >= NLON, s - NLON, s)

    def turn(c, s, c1, s1):
        return c * c1 - s * s1, s * c1 + c * s1

    tile = min(64, orows)
    base = min(lanes, part_m)
    for h in range(2):
        def along_m(i, carry):
            here = pl.ds(pl.multiple_of(i * tile, tile), tile)
            lon = longitude(spot_col[h, here, pl.ds(0, base)])
            c, s = cos_sin(lon * (waves * iota((tile, base), 1)).astype(F32), NLON)
            by_one = cos_sin(lon, NLON)
            by_base = cos_sin(lon * float(waves * base), NLON)
            for w in range(waves):
                if w > 0:
                    c, s = turn(*first, *by_one)
                first = (c, s)
                for q in range(part_m // base):
                    table[h, here, pl.ds(2 * w * part_m + q * base, base)] = c.astype(BF16)
                    table[h, here, pl.ds((2 * w + 1) * part_m + q * base, base)] = s.astype(BF16)
                    c, s = turn(c, s, *by_base)
            return carry

        lax.fori_loop(0, orows // tile, along_m, 0)

    deep = min(64, part_m)
    wide = min(128, orows)
    for h in range(2):
        def along_o(i, carry):
            here = pl.ds(pl.multiple_of(i * wide, wide), wide)
            there = [pl.ds(pl.multiple_of((2 * h + k) * orows + i * wide, wide), wide) for k in range(2)]
            lon = longitude(spot_row[h, pl.ds(0, deep), here])
            c, s = cos_sin(lon * (waves * iota((deep, wide), 0)).astype(F32), NLON)
            by_one = cos_sin(lon, NLON)
            by_deep = cos_sin(lon * float(waves * deep), NLON)
            for w in range(waves):
                if w > 0:
                    c, s = turn(*first, *by_one)
                first = (c, s)
                for q in range(part_m // deep):
                    flipped[pl.ds(w * part_m + q * deep, deep), there[0]] = c.astype(BF16)
                    flipped[pl.ds(w * part_m + q * deep, deep), there[1]] = s.astype(BF16)
                    c, s = turn(c, s, *by_deep)
            return carry

        lax.fori_loop(0, orows // wide, along_o, 0)

    scale = 1.0 / math.sqrt(total_m)
    vc = jnp.concatenate([vcoef_ref[:, 0, :]] * 4, axis=1) * scale
    lev_row = lax.rem(iota((lanes, lanes), 0), levels)
    lev_col = lax.rem(iota((lanes, lanes), 1), levels)
    up = jnp.zeros((lanes, lanes), F32)
    for k in range(band):
        up = up + jnp.where(lev_row == lev_col + (k - half), vc[k : k + 1, :], 0.0)
    col_chunk = lax.div(iota((lanes, lanes), 1), levels)
    row_chunk = lax.div(iota((lanes, lanes), 0), levels)
    ups = jnp.where(lax.div(row_chunk, 2) * 2 == col_chunk, up, 0.0)
    downs = jnp.concatenate([jnp.where(col_chunk == 2 * h, up, 0.0) for h in range(2)], axis=0)
    chunk_o = lax.div(lane, levels)
    got32 = got.astype(F32)
    weight = pltpu.roll(got32, lanes - levels, 1)
    weight = jnp.where(lax.rem(chunk_o, 2) == 0, weight, 0.0)

    def split(x):
        coarse = x.astype(BF16)
        return coarse, (x - coarse.astype(F32)).astype(BF16)

    def dot3(a, split_b, dims):
        a0, a1 = split(a)
        b0, b1 = split_b
        return dot(a0, b0, dims) + (dot(a1, b0, dims) + dot(a0, b1, dims))

    ups, downs = split(ups), split(downs)
    at_lat = [lax.rem(chunk_o, 2) == (spot_col[h] >= NLON).astype(jnp.int32) for h in range(2)]

    grids = [jnp.zeros((orows, lanes), F32) for h in range(2)]
    for w in range(waves):
        recv_all(w, *stage_b)
        four = recv_b[w].reshape(part_m, lanes)
        crossed = pltpu.roll(four.astype(F32), lanes // 2, 1).astype(BF16)
        sides = (jnp.concatenate([four, crossed], axis=0), jnp.concatenate([crossed, four], axis=0))
        for h in range(2):
            grids[h] = grids[h] + dot(table[h, :, pl.ds(2 * w * part_m, 2 * part_m)], sides[h])
    grids = [jnp.where(at_lat[h], grids[h], 0.0) for h in range(2)]
    grid = jnp.where(chunk_o < 2, grids[0], grids[1])
    weighted = weight * (dot3(grid, ups, (1, 0)) - got32)
    backs = dot3(weighted, downs, (1, 1))
    columns = []
    for h in range(2):
        back = jnp.where(at_lat[h], backs[:, h * lanes : (h + 1) * lanes], 0.0)
        columns += [jnp.where(chunk_o < 2, back, 0.0).astype(BF16), jnp.where(chunk_o < 2, 0.0, back).astype(BF16)]
    columns = jnp.concatenate(columns, axis=0)
    for w in range(waves):
        wave = dot(flipped[pl.ds(w * part_m, part_m), :], columns)
        send_c[w] = wave.astype(BF16).reshape(send_c.shape[1:])
        start_all(w, *stage_c)
    for w in range(waves):
        turned_ref[w] = leg[w].T
    store_turned = pltpu.make_async_copy(turned_ref, turned_hbm, store_sem.at[waves])
    store_turned.start()
    for w in range(waves):
        recv_all(w, *stage_c)
        swap(w, recv_c, send_d, nxz, group)
        start_all(w, *stage_d)

    stores = []
    for w in range(waves):
        recv_all(w, *stage_d)
        for yy in range(ny):
            parts = [recv_d[w, yy * nfld + ff].astype(F32) for ff in range(nfld)]
            for r in range(2):
                for j in range(2):
                    k = 2 * r + j
                    out = parts[0] if k == 0 else pltpu.roll(parts[0], (0 - k) % 4 * levels, 1)
                    for ff in range(1, nfld):
                        moved = parts[ff] if ff == k else pltpu.roll(parts[ff], (ff - k) % 4 * levels, 1)
                        out = jnp.where(chunk == ff, moved, out)
                    rows_f[pl.ds((r * waves + w) * lat + 2 * yy + j, nxz, stride=2 * ny), :] = out
        for r in range(2):
            rows = rows_f[pl.ds((r * waves + w) * lat, lat), :]
            wave_ref[w, :, pl.ds(r * lanes, lanes)] = rows.astype(BF16)
        stores.append(pltpu.make_async_copy(wave_ref.at[w], wave_hbm.at[w], store_sem.at[w]))
        stores[w].start()

    send_done(0, *obs_xz)
    send_done(0, *obs_y)
    for w in range(waves):
        for stage in (stage_a, stage_b, stage_c, stage_d):
            send_done(w, *stage)
    store_turned.wait()
    for store in stores:
        store.wait()


def on_device(coef, leg, vcoef, obs_value, obs_weight, obs_dest, obs_spot, obs_count, ny=NY):
    nblk = lax.axis_size("blk")
    nfld = lax.axis_size("fld")
    waves, lat, nn = leg.shape
    width = coef.shape[2]
    levels = vcoef.shape[2]
    lanes = 4 * levels
    nxz = nblk // ny
    group = ny * nfld
    part_m = nxz * group
    total_m = waves * part_m
    orows = nblk * SLOT_ROWS
    obs_dev = obs_spot.shape[0]

    def buffer(*shape):
        return pltpu.VMEM(shape, BF16)

    hbm = pl.BlockSpec(memory_space=pltpu.HBM)
    band_shape = (vcoef.shape[1], 1, levels)
    scratch = [
        buffer(waves, lat, width), buffer(waves, nn, lat),
        buffer(waves, lat, nn), buffer(waves, nn, width), pltpu.VMEM(band_shape, F32),
        buffer(levels, obs_dev), pltpu.VMEM((levels, obs_dev), F32), pltpu.VMEM((1, obs_dev), jnp.int32),
        pltpu.VMEM((1, obs_dev), jnp.int32), pltpu.VMEM((2 * waves * lat, lanes), F32),
        pltpu.VMEM((orows, lanes), F32),
        buffer(waves, group, nxz, lanes), buffer(waves, group, nxz, lanes),
        buffer(waves, nxz, group, lanes), buffer(waves, nxz, group, lanes),
        buffer(1, ny, nxz * SLOT_ROWS, lanes), buffer(1, ny, nxz * SLOT_ROWS, lanes),
        buffer(1, nxz, ny * SLOT_ROWS, lanes), buffer(1, nxz, ny * SLOT_ROWS, lanes),
        buffer(waves, nxz, group, lanes), buffer(waves, nxz, group, lanes),
        buffer(waves, group, nxz, lanes), buffer(waves, group, nxz, lanes),
        pltpu.VMEM((2, orows, lanes), F32), pltpu.VMEM((2, lanes, orows), F32),
        buffer(2, orows, 2 * total_m), buffer(total_m, 4 * orows),
        pltpu.SemaphoreType.DMA((7,)), pltpu.SemaphoreType.DMA((waves + 1,)),
    ]
    for parts in (waves, waves, 1, 1, waves, waves):
        scratch += [pltpu.SemaphoreType.DMA((parts,)), pltpu.SemaphoreType.DMA((parts,))]
    wave, turned = pl.pallas_call(
        functools.partial(kernel, nblk, nfld, ny),
        out_shape=(
            jax.ShapeDtypeStruct((waves, lat, width), BF16),
            jax.ShapeDtypeStruct((waves, nn, lat), BF16),
        ),
        in_specs=[hbm] * 7 + [pl.BlockSpec(memory_space=pltpu.SMEM)],
        out_specs=(hbm, hbm),
        scratch_shapes=scratch,
        compiler_params=pltpu.CompilerParams(
            collective_id=0, has_side_effects=True, vmem_limit_bytes=60 * 1024 * 1024
        ),
    )(
        leg, coef, vcoef.reshape(band_shape), obs_value[0], obs_weight[0], obs_dest.reshape(1, obs_dev),
        obs_spot.reshape(1, obs_dev), obs_count,
    )
    return jnp.einsum("mnj,mjc->mnc", turned, wave, preferred_element_type=F32).astype(BF16)


def solution(mesh):
    in_specs = (
        P(("blk", "fld"), None, None),
        P(("blk", "fld"), None, None),
        P("fld", None, None),
        P("fld", None, "blk"),
        P("fld", None, "blk"),
        P("blk", None),
        P("blk"),
        P("blk"),
    )
    out_specs = P(("blk", "fld"), None, None)
    return jax.shard_map(
        on_device, mesh=mesh, in_specs=in_specs, out_specs=out_specs, check_vma=False
    )
```

time: 82.1 us -> 67.5 us (0.82)
  Pallas kernels: 72.8 us -> 63.8 us
  local copies, waits for them, and re-layouts: 7.72 us -> 0 us
  matrix products: 0.56 us -> 2.9 us
    pallas_call x1, Pallas kernels: 72.8 us -> 63.8 us  [on_device(): pl.pallas_call(functools.partial(kernel, nblk, nfld, ny), out_shape=(jax....]
    unnamed x13 -> x0, local copies, waits for them, and re-layouts: 6.28 us -> none
    dot_general x1, matrix products: 0.56 us -> 2.9 us  [on_device(): jnp.einsum('mnj,mjc->mnc', turned, wave, preferred_element_type=F32)]
    convert_element_type x1 -> x0, local copies, waits for them, and re-layouts: 1.44 us -> none  [on_device(): jnp.einsum('mjn,mjc->mnc', leg, wave, preferred_element_type=F32)]
where the time goes in v2:
time: 67.5 us; the launch traced here: 67.3 us
  Pallas kernels  63.8 us (95%)
  matrix products  2.9 us (4%)
    pallas_call x1, Pallas kernels, on_device(): pl.pallas_call(functools.partial(kernel, nblk, nfld, ny), out_shape=(jax....  63.8 us
    dot_general x1, matrix products, on_device(): jnp.einsum('mnj,mjc->mnc', turned, wave, preferred_element_type=F32)  2.9 us

profile of v2, /device:TPU:1, one launch (start us, length us, event | category | flops | bytes accessed | tf_op | source)
XLA Modules:
  0.0 67.3 jit_solution(653036157328759390)
XLA Ops:
  0.7 63.8 %shard_map.82 = (bf16[2,256,256]{2,1,0:T(8,128)(2,1)}, bf16[2,1280,256]{2,1,0:T(8,128)(2,1)}) custom-call(bf16[2,256,1280]{2,1,0:T(8,128)(2,1)} %leg_hbm.1, bf16[2,1280,256]{2,1,0:T(8,128)(2,1)} %coef_hbm.1, f32[7,1,32]{2,1,0:T(1,128)} %bitcast.9, bf16[32,512]{1,0:T(8,128)(2,1)} %bitcast.8, f32[32,512]{1,0:T(8,128)} %bitcast.7, s32[1,512]{1,0:T(1,128)} %bitcast.10, ...), custom_call_target="tpu_custom_call" | custom-call | tf_op jit(solution)/shard_map/pallas_call | solution.py:428
  64.4 2.9 %convolution_convert_fusion = bf16[2,1280,256]{2,1,0:T(8,128)(2,1)} fusion(bf16[2,1280,256]{2,1,0:T(8,128)(2,1)} %get-tuple-element.7, bf16[2,256,256]{2,1,0:T(8,128)(2,1)} %get-tuple-element.8), kind=kOutput, calls=%fused_computation | convolution fusion | flops 336199680 | bytes 2883584 | tf_op jit(solution)/shard_map/mnj,mjc->mnc/dot_general | solution.py:444

commit v3 on v2

v3 whole, which is shorter than its diff:
```python
import functools
import math

import jax
import jax.numpy as jnp
import numpy as np
from jax import lax
from jax.experimental import pallas as pl
from jax.experimental.pallas import tpu as pltpu
from jax.sharding import PartitionSpec as P

NLON = 2560
NY = 4
SLOT_ROWS = 4
MESH = pl.DeviceIdType.MESH
F32 = jnp.float32
BF16 = jnp.bfloat16


def power_series(f, terms):
    fit = np.polynomial.chebyshev.Chebyshev.interpolate(f, terms - 1, domain=[0.0, 0.25])
    return [float(c) for c in fit.convert(kind=np.polynomial.Polynomial).coef]


def cos_series():
    return power_series(lambda v: np.cos(2 * np.pi * np.sqrt(v)), 7)


def sin_series():
    return power_series(lambda v: 2 * np.pi * np.sinc(2 * np.sqrt(v)), 7)


def horner(coefs, v):
    total = jnp.full_like(v, coefs[-1])
    for c in coefs[-2::-1]:
        total = total * v + c
    return total


def cos_sin(turns, whole):
    rest = turns - jnp.round(turns * (1.0 / whole)) * whole
    u = rest * (1.0 / whole)
    v = u * u
    return horner(cos_series(), v), u * horner(sin_series(), v)


def dot(a, b, dims=(1, 0), precision=None):
    return lax.dot_general(
        a, b, (((dims[0],), (dims[1],)), ((), ())), precision=precision, preferred_element_type=F32
    )


def iota(shape, axis):
    return lax.broadcasted_iota(jnp.int32, shape, axis)


def kernel(
    nblk, nfld, ny, leg_hbm, coef_hbm, vcoef_hbm, val_hbm, wgt_hbm, dest_hbm, spot_hbm, count_ref, out_hbm,
    out, turned, leg, coef, vcoef_ref, val_ref, wgt_ref, dest_ref, spot_ref, rows_f, tmp_o, send_a, recv_a, send_b, recv_b, send_oa, recv_oa, send_ob, recv_ob,
    send_c, recv_c, send_d, recv_d, spot_col, spot_row, table, alpha, flipped,
    load_sem, store_sem, sa_s, sa_r, sb_s, sb_r, oa_s, oa_r, ob_s, ob_r, sc_s, sc_r, sd_s, sd_r,
):
    nxz = nblk // ny
    nz = nxz // 2
    group = ny * nfld
    waves, lat = leg.shape[0], leg.shape[1]
    part_m = nxz * group
    total_m = waves * part_m
    levels = vcoef_ref.shape[2]
    band = vcoef_ref.shape[0]
    half = (band - 1) // 2
    lanes = 4 * levels
    obs_dev = dest_ref.shape[1]
    orows = nblk * SLOT_ROWS
    slots = nblk * (SLOT_ROWS - 1)

    b = lax.axis_index("blk")
    f = lax.axis_index("fld")
    y = lax.rem(b, ny)
    xz = lax.div(b, ny)
    member = y * nfld + f

    x_hi = lax.div(xz, nz)
    z = lax.rem(xz, nz)

    def each_xz(act):
        for flip in (1, 0):
            plane = lax.rem(x_hi + flip, 2) * nz
            act(plane + lax.rem(z + nz // 2, nz))

            def step(i, carry):
                act(plane + lax.rem(z + nz // 2 - i, nz))
                act(plane + lax.rem(z + nz - nz // 2 + i, nz))
                return carry

            lax.fori_loop(1, nz // 2, step, 0)
            if flip:
                act(plane + z)

    def each_of(mine, count):
        def each(act):
            def step(i, carry):
                act(lax.rem(mine + i, count))
                return carry

            lax.fori_loop(1, count, step, 0)

        return each

    def group_device(mem):
        return (xz * ny + lax.div(mem, nfld), lax.rem(mem, nfld))

    def xz_device(other):
        return (other * ny + y, f)

    def y_device(other):
        return (xz * ny + other, f)

    def start_all(part, count, each, device, mine, src, dst, send_sem, recv_sem):
        def start(other):
            pltpu.make_async_remote_copy(
                src_ref=src.at[part, other], dst_ref=dst.at[part, mine], send_sem=send_sem.at[part],
                recv_sem=recv_sem.at[part], device_id=device(other), device_id_type=MESH,
            ).start()

        each(start)
        dst[part, mine] = src[part, mine]

    def whole(part, count, each, device, mine, src, dst, send_sem, recv_sem):
        others = pl.ds(0, count - 1)
        return pltpu.make_async_remote_copy(
            src_ref=src.at[part, others], dst_ref=dst.at[part, others], send_sem=send_sem.at[part],
            recv_sem=recv_sem.at[part], device_id=device(lax.rem(mine + 1, count)), device_id_type=MESH,
        )

    def recv_all(part, *stage):
        whole(part, *stage).wait_recv()

    def send_done(part, *stage):
        whole(part, *stage).wait_send()

    in_group = (group, each_of(member, group), group_device, member)
    in_xz = (nxz, each_xz, xz_device, xz)
    in_y = (ny, each_of(y, ny), y_device, y)
    stage_a = (*in_group, send_a, recv_a, sa_s, sa_r)
    stage_b = (*in_xz, send_b, recv_b, sb_s, sb_r)
    stage_c = (*in_xz, send_c, recv_c, sc_s, sc_r)
    stage_d = (*in_group, send_d, recv_d, sd_s, sd_r)
    obs_xz = (*in_xz, send_ob, recv_ob, ob_s, ob_r)
    obs_y = (*in_y, send_oa, recv_oa, oa_s, oa_r)

    loads = [
        pltpu.make_async_copy(src, dst, load_sem.at[i])
        for i, (src, dst) in enumerate(
            (
                (dest_hbm, dest_ref), (spot_hbm, spot_ref), (val_hbm, val_ref), (wgt_hbm, wgt_ref),
                (vcoef_hbm, vcoef_ref), (coef_hbm, coef), (leg_hbm, leg),
            )
        )
    ]
    for load in loads:
        load.start()
    barrier = pltpu.get_barrier_semaphore()

    def greet(count, each, device, mine):
        def tell(other):
            pl.semaphore_signal(barrier, inc=1, device_id=device(other), device_id_type=MESH)

        each(tell)

    greet(*in_xz)
    greet(*in_group)
    for load in loads[:5]:
        load.wait()

    dest = dest_ref[...]
    spot = spot_ref[...]
    live = iota((1, obs_dev), 1) < count_ref[0]
    place = jnp.where(live, lax.rem(dest, ny) * nxz + lax.div(dest, ny), -1)
    onehot = (iota((nblk, obs_dev), 0) == place).astype(BF16)
    part = min(128, obs_dev)
    upto = iota((part, 2 * part), 0) < iota((part, 2 * part), 1)
    ranks = []
    carry = jnp.zeros((nblk, part), F32)
    for i in range(obs_dev // part):
        piece = onehot[:, i * part : (i + 1) * part]
        counted = dot(piece, upto.astype(BF16))
        ranks.append(jnp.sum((counted[:, :part] + carry) * piece.astype(F32), axis=0, keepdims=True))
        carry = carry + counted[:, part:]
    rank = jnp.concatenate(ranks, axis=1).astype(jnp.int32)
    data = jnp.concatenate([val_ref[...].astype(F32), wgt_ref[...]], axis=0)
    lane_q = iota((lanes, obs_dev), 0)
    high = lax.div(spot, 32)
    low = spot - high * 32
    spots = jnp.where(lane_q == rank, high, jnp.where(lane_q == rank + 8, low, 0)).astype(F32)
    for k in range(SLOT_ROWS):
        rows = spots
        if k < SLOT_ROWS - 1:
            rows = [jnp.where(rank == 2 * k + h, data, 0.0) for h in range(2)]
            rows = jnp.concatenate(rows, axis=0)
        packed = dot(onehot, rows.astype(BF16), (1, 1))
        for yy in range(ny):
            tmp_o[pl.ds(yy * SLOT_ROWS + k, nxz, stride=ny * SLOT_ROWS), :] = packed[yy * nxz : (yy + 1) * nxz]
    send_ob[...] = tmp_o[...].astype(BF16).reshape(send_ob.shape)

    chunk = lax.div(iota((nxz, lanes), 1), levels)

    def pack(j):
        for yy in range(ny):
            parts = [
                rows_f[pl.ds((r * waves + w) * lat + 2 * yy + j, nxz, stride=2 * ny), :]
                for w in range(waves)
                for r in range(2)
            ]
            for ff in range(nfld):
                merged = parts[0] if ff == 0 else pltpu.roll(parts[0], (0 - ff) % 4 * levels, 1)
                for k in range(1, 4):
                    moved = parts[k] if ff == k else pltpu.roll(parts[k], (k - ff) % 4 * levels, 1)
                    merged = jnp.where(chunk == k, moved, merged)
                send_a[j, yy * nfld + ff] = merged.astype(BF16)

    def swap(part, src, dst, outer, inner):
        tmp_o[...] = src[part].astype(F32).reshape(tmp_o.shape)
        per = dst.shape[2] // outer
        for i in range(inner):
            rows = tmp_o[pl.ds(i, outer, stride=inner), :]
            dst[part, i // per, pl.ds(i % per * outer, outer), :] = rows.astype(BF16)

    for load in loads[5:]:
        load.wait()
    for w in range(waves):
        result = dot(leg[w], coef[w])
        for r in range(2):
            rows_f[pl.ds((r * waves + w) * lat, lat), :] = result[:, r * lanes : (r + 1) * lanes]
    pack(0)
    pl.semaphore_wait(barrier, group - 1 + nxz - 1)
    start_all(0, *stage_a)
    start_all(0, *obs_xz)
    pack(1)
    start_all(1, *stage_a)

    for j in range(2):
        recv_all(j, *stage_a)
        swap(j, recv_a, send_b, group, nxz)
        start_all(j, *stage_b)

    recv_all(0, *obs_xz)
    swap(0, recv_ob, send_oa, nxz, ny * SLOT_ROWS)
    start_all(0, *obs_y)
    recv_all(0, *obs_y)

    got = [recv_oa[0, yy, pl.ds(0, (SLOT_ROWS - 1) * nxz), :] for yy in range(ny)]
    got = jnp.concatenate(got, axis=0)
    spread = [recv_oa[0, yy, pl.ds((SLOT_ROWS - 1) * nxz, nxz), :] for yy in range(ny) for k in range(SLOT_ROWS - 1)]
    spread = jnp.concatenate(spread, axis=0).astype(F32)
    lane = iota((slots, lanes), 1)
    k_row = lax.rem(lax.div(iota((slots, lanes), 0), nxz), SLOT_ROWS - 1)
    for h in range(2):
        q = 2 * k_row + h
        mine = jnp.where(lane == q, spread * 32.0, jnp.where(lane == q + 8, spread, 0.0)).astype(BF16)
        spot_col[h] = dot(mine, jnp.ones((lanes, lanes), BF16))
        spot_row[h] = dot(jnp.ones((8, lanes), BF16), mine, (1, 1))

    def longitude(s):
        return jnp.where(s >= NLON, s - NLON, s)

    def turn(c, s, c1, s1):
        return c * c1 - s * s1, s * c1 + c * s1

    base = part_m // 4
    far = 2 * lanes
    tile = min(64, slots)
    for h in range(2):
        def along_m(i, carry):
            here = pl.ds(pl.multiple_of(i * tile, tile), tile)
            there = pl.ds(pl.multiple_of(h * slots + i * tile, tile), tile)
            lon = longitude(spot_col[h, here, :])
            for t in range(2):
                col = iota((tile, lanes), 1)
                step = lax.div(col, 2 * levels) + 2 * t
                quarter = lax.rem(lax.div(col, levels), 2) * (NLON // 4)
                phase = lon * (2 * base * step).astype(F32) - quarter.astype(F32)
                alpha[there, pl.ds(t * lanes, lanes)] = cos_sin(phase, NLON)[0]
            lon = lon[:, :base]
            odd = cos_sin(lon * (2 * iota((tile, base), 1) + 1).astype(F32), NLON)
            one = [jnp.broadcast_to(x[:, :1], x.shape) for x in odd]
            for w, pair in enumerate((turn(*odd, one[0], 0.0 - one[1]), odd)):
                for k in range(2):
                    table[there, pl.ds((2 * w + k) * base, base)] = pair[k].astype(BF16)
            return carry

        lax.fori_loop(0, slots // tile, along_m, 0)

    deep = min(64, base)
    wide = min(128, slots)
    for h in range(2):
        def along_o(i, carry):
            here = pl.ds(pl.multiple_of(i * wide, wide), wide)
            there = pl.ds(pl.multiple_of(h * slots + i * wide, wide), wide)
            lon = longitude(spot_row[h, :, here])
            one = [x[:1] for x in cos_sin(lon, NLON)]
            for q in range(base // deep):
                odd = cos_sin(lon[:1] * (2 * (iota((deep, wide), 0) + q * deep) + 1).astype(F32), NLON)
                for w, pair in enumerate((turn(*odd, one[0], 0.0 - one[1]), odd)):
                    for k in range(2):
                        flipped[pl.ds((2 * w + k) * base + q * deep, deep), there] = pair[k].astype(BF16)
            return carry

        lax.fori_loop(0, slots // wide, along_o, 0)

    scale = 1.0 / math.sqrt(total_m)
    vc = jnp.concatenate([vcoef_ref[:, 0, :]] * 4, axis=1) * scale
    lev_row = lax.rem(iota((lanes, lanes), 0), levels)
    lev_col = lax.rem(iota((lanes, lanes), 1), levels)
    up = jnp.zeros((lanes, lanes), F32)
    for k in range(band):
        up = up + jnp.where(lev_row == lev_col + (k - half), vc[k : k + 1, :], 0.0)
    col_chunk = lax.div(iota((lanes, lanes), 1), levels)
    ups = jnp.concatenate([jnp.where(col_chunk == 2 * h, up, 0.0) for h in (0, 0, 1, 1)], axis=0)
    chunk_o = lax.div(lane, levels)
    got32 = got.astype(F32)
    weight = pltpu.roll(got32, lanes - levels, 1)
    weight = jnp.where(lax.rem(chunk_o, 2) == 0, weight, 0.0)

    def split(x):
        coarse = x.astype(BF16)
        return coarse, (x - coarse.astype(F32)).astype(BF16)

    def dot3(a, split_b, dims):
        a0, a1 = split(a)
        b0, b1 = split_b
        return dot(a0, b0, dims) + (dot(a1, b0, dims) + dot(a0, b1, dims))

    ups = split(ups)
    latitude = jnp.where(chunk_o < 2, spot_col[0], spot_col[1]) >= NLON

    near_lane = iota((base, lanes), 1)
    low = near_lane < lanes // 2
    even = lax.rem(lax.div(near_lane, levels), 2) == 0

    for j in range(2):
        recv_all(j, *stage_b)
        four = recv_b[j].reshape(part_m, lanes).astype(F32)
        near = [four[a * base : (a + 1) * base] for a in range(4)]
        moved = [pltpu.roll(x, lanes // 2, 1) for x in near]
        sides = []
        for w in range(2):
            kept, other = (near, moved) if w == 0 else (moved, near)
            tops = [jnp.where(low, kept[2 * t], other[2 * t + 1]) for t in range(2)]
            sides.append(jnp.concatenate(tops, axis=1))
            crossed = [
                jnp.where(even, pltpu.roll(x, lanes - levels, 1), 0.0 - pltpu.roll(x, levels, 1)) for x in tops
            ]
            sides.append(jnp.concatenate(crossed, axis=1))
        grid = dot(table[...], jnp.concatenate(sides, axis=0).astype(BF16)) * alpha[...]
        grid = jnp.concatenate([grid[:slots], grid[slots:]], axis=1)
        here = latitude if j else jnp.logical_not(latitude)
        weighted = jnp.where(here, weight * (dot3(grid, ups, (1, 0)) - got32), 0.0)
        backs = dot3(weighted, ups, (1, 1))
        backs = jnp.concatenate([backs[:, :far], backs[:, far:]], axis=0) * alpha[...]
        sums = dot(flipped[...], backs.astype(BF16))
        mixed = []
        for w in range(2):
            by_cos, by_sin = [sums[(2 * w + k) * base : (2 * w + k + 1) * base] for k in range(2)]
            for t in range(2):
                x = by_sin[:, t * lanes : (t + 1) * lanes]
                x = jnp.where(even, 0.0 - pltpu.roll(x, lanes - levels, 1), pltpu.roll(x, levels, 1))
                mixed.append(by_cos[:, t * lanes : (t + 1) * lanes] + x)
        wave = []
        for t in range(2):
            first, second = mixed[t], mixed[2 + t]
            wave.append(jnp.where(low, first, pltpu.roll(second, lanes // 2, 1)))
            wave.append(jnp.where(low, pltpu.roll(first, lanes // 2, 1), second))
        wave = jnp.concatenate(wave, axis=0)
        send_c[j] = wave.astype(BF16).reshape(send_c.shape[1:])
        start_all(j, *stage_c)
        turned[j] = leg[j].T

    for j in range(2):
        recv_all(j, *stage_c)
        swap(j, recv_c, send_d, nxz, group)
        start_all(j, *stage_d)
    for j in range(2):
        recv_all(j, *stage_d)
        for yy in range(ny):
            parts = [recv_d[j, yy * nfld + ff].astype(F32) for ff in range(nfld)]
            for w in range(waves):
                for r in range(2):
                    k = 2 * w + r
                    merged = parts[0] if k == 0 else pltpu.roll(parts[0], (0 - k) % 4 * levels, 1)
                    for ff in range(1, nfld):
                        moved = parts[ff] if ff == k else pltpu.roll(parts[ff], (ff - k) % 4 * levels, 1)
                        merged = jnp.where(chunk == ff, moved, merged)
                    rows_f[pl.ds((r * waves + w) * lat + 2 * yy + j, nxz, stride=2 * ny), :] = merged
    stores = []
    for w in range(waves):
        wave = [rows_f[pl.ds((r * waves + w) * lat, lat), :].astype(BF16) for r in range(2)]
        out[w] = dot(turned[w], jnp.concatenate(wave, axis=1)).astype(BF16)
        stores.append(pltpu.make_async_copy(out.at[w], out_hbm.at[w], store_sem.at[w]))
        stores[w].start()

    send_done(0, *obs_xz)
    send_done(0, *obs_y)
    for j in range(2):
        for stage in (stage_a, stage_b, stage_c, stage_d):
            send_done(j, *stage)
    for store in stores:
        store.wait()


def on_device(coef, leg, vcoef, obs_value, obs_weight, obs_dest, obs_spot, obs_count, ny=NY):
    nblk = lax.axis_size("blk")
    nfld = lax.axis_size("fld")
    waves, lat, nn = leg.shape
    width = coef.shape[2]
    levels = vcoef.shape[2]
    lanes = 4 * levels
    nxz = nblk // ny
    group = ny * nfld
    part_m = nxz * group
    total_m = waves * part_m
    orows = nblk * SLOT_ROWS
    slots = nblk * (SLOT_ROWS - 1)
    obs_dev = obs_spot.shape[0]

    def buffer(*shape):
        return pltpu.VMEM(shape, BF16)

    hbm = pl.BlockSpec(memory_space=pltpu.HBM)
    band_shape = (vcoef.shape[1], 1, levels)
    scratch = [
        buffer(waves, nn, width), buffer(waves, nn, lat),
        buffer(waves, lat, nn), buffer(waves, nn, width), pltpu.VMEM(band_shape, F32),
        buffer(levels, obs_dev), pltpu.VMEM((levels, obs_dev), F32), pltpu.VMEM((1, obs_dev), jnp.int32),
        pltpu.VMEM((1, obs_dev), jnp.int32), pltpu.VMEM((2 * waves * lat, lanes), F32),
        pltpu.VMEM((orows, lanes), F32),
        buffer(2, group, nxz, lanes), buffer(2, group, nxz, lanes),
        buffer(2, nxz, group, lanes), buffer(2, nxz, group, lanes),
        buffer(1, ny, nxz * SLOT_ROWS, lanes), buffer(1, ny, nxz * SLOT_ROWS, lanes),
        buffer(1, nxz, ny * SLOT_ROWS, lanes), buffer(1, nxz, ny * SLOT_ROWS, lanes),
        buffer(2, nxz, group, lanes), buffer(2, nxz, group, lanes),
        buffer(2, group, nxz, lanes), buffer(2, group, nxz, lanes),
        pltpu.VMEM((2, slots, lanes), F32), pltpu.VMEM((2, 8, slots), F32),
        buffer(2 * slots, part_m), pltpu.VMEM((2 * slots, 2 * lanes), F32), buffer(part_m, 2 * slots),
        pltpu.SemaphoreType.DMA((7,)), pltpu.SemaphoreType.DMA((waves,)),
    ]
    for parts in (2, 2, 1, 1, 2, 2):
        scratch += [pltpu.SemaphoreType.DMA((parts,)), pltpu.SemaphoreType.DMA((parts,))]
    return pl.pallas_call(
        functools.partial(kernel, nblk, nfld, ny),
        out_shape=jax.ShapeDtypeStruct((waves, nn, width), BF16),
        in_specs=[hbm] * 7 + [pl.BlockSpec(memory_space=pltpu.SMEM)],
        out_specs=hbm,
        scratch_shapes=scratch,
        compiler_params=pltpu.CompilerParams(
            collective_id=0, has_side_effects=True, vmem_limit_bytes=60 * 1024 * 1024
        ),
    )(
        leg, coef, vcoef.reshape(band_shape), obs_value[0], obs_weight[0], obs_dest.reshape(1, obs_dev),
        obs_spot.reshape(1, obs_dev), obs_count,
    )

def solution(mesh):
    in_specs = (
        P(("blk", "fld"), None, None),
        P(("blk", "fld"), None, None),
        P("fld", None, None),
        P("fld", None, "blk"),
        P("fld", None, "blk"),
        P("blk", None),
        P("blk"),
        P("blk"),
    )
    out_specs = P(("blk", "fld"), None, None)
    return jax.shard_map(
        on_device, mesh=mesh, in_specs=in_specs, out_specs=out_specs, check_vma=False
    )
```

time: 67.5 us -> 62.2 us (0.921)
  Pallas kernels: 63.8 us -> 58.9 us
  matrix products: 2.9 us -> 0 us
  local copies, waits for them, and re-layouts: 0 us -> 2.46 us
    pallas_call x1, Pallas kernels: 63.8 us -> 58.9 us  [on_device(): pl.pallas_call(functools.partial(kernel, nblk, nfld, ny), out_shape=jax.S...]
    dot_general x1 -> x0, matrix products: 2.9 us -> none  [on_device(): jnp.einsum('mnj,mjc->mnc', turned, wave, preferred_element_type=F32)]
    unnamed x0 -> x1, local copies, waits for them, and re-layouts: none -> 2.46 us
where the time goes in v3:
time: 62.2 us; the launch traced here: 62 us
  Pallas kernels  58.9 us (95%)
  local copies, waits for them, and re-layouts  2.46 us (4%)
  between operations  0.66 us (1%)
    pallas_call x1, Pallas kernels, on_device(): pl.pallas_call(functools.partial(kernel, nblk, nfld, ny), out_shape=jax.S...  58.9 us
    unnamed x1, local copies, waits for them, and re-layouts  2.46 us

profile of v3, /device:TPU:1, one launch (start us, length us, event | category | flops | bytes accessed | tf_op | source)
XLA Modules:
  0.0 62.0 jit_solution(5857318816940471940)
XLA Ops:
  0.7 58.9 %shard_map.82 = bf16[2,1280,256]{2,1,0:T(8,128)(2,1)} custom-call(bf16[2,256,1280]{2,1,0:T(8,128)(2,1)} %leg_hbm.1, bf16[2,1280,256]{2,1,0:T(8,128)(2,1)} %coef_hbm.1, f32[7,1,32]{2,1,0:T(1,128)} %bitcast.7, bf16[32,512]{1,0:T(8,128)(2,1)} %bitcast.6, f32[32,512]{1,0:T(8,128)} %bitcast.5, s32[1,512]{1,0:T(1,128)} %bitcast.8, s32[1,512]{1,0:T(1,128)} %bitcast.9, ...), custom_call_target="tpu_custom_call" | custom-call | tf_op jit(solution)/shard_map/pallas_call | solution.py:449
  59.6 2.5 %copy.11 = bf16[2,1280,256]{2,1,0:T(8,128)(2,1)} copy(bf16[2,1280,256]{2,1,0:T(8,128)(2,1)} %shard_map.82) | data formatting | bytes 2621440

commit v4 on v3

--- a/solution.py
+++ b/solution.py
@@ -55,8 +55,8 @@
 
 
 def kernel(
-    nblk, nfld, ny, leg_hbm, coef_hbm, vcoef_hbm, val_hbm, wgt_hbm, dest_hbm, spot_hbm, count_ref, out_hbm,
-    out, turned, leg, coef, vcoef_ref, val_ref, wgt_ref, dest_ref, spot_ref, rows_f, tmp_o, send_a, recv_a, send_b, recv_b, send_oa, recv_oa, send_ob, recv_ob,
+    nblk, nfld, ny, leg_hbm, coef_hbm, vcoef_hbm, val_hbm, wgt_hbm, dest_hbm, spot_hbm, count_ref, wave_hbm, turned_hbm,
+    wave_ref, turned, leg, coef, vcoef_ref, val_ref, wgt_ref, dest_ref, spot_ref, rows_f, tmp_o, send_a, recv_a, send_b, recv_b, send_oa, recv_oa, send_ob, recv_ob,
     send_c, recv_c, send_d, recv_d, spot_col, spot_row, table, alpha, flipped,
     load_sem, store_sem, sa_s, sa_r, sb_s, sb_r, oa_s, oa_r, ob_s, ob_r, sc_s, sc_r, sd_s, sd_r,
 ):
@@ -158,18 +158,22 @@
             )
         )
     ]
-    for load in loads:
+    barrier = pltpu.get_barrier_semaphore()
+
+    def tell(device, other):
+        pl.semaphore_signal(barrier, inc=1, device_id=device(other), device_id_type=MESH)
+
+    for load in loads[5:]:
         load.start()
-    barrier = pltpu.get_barrier_semaphore()
-
-    def greet(count, each, device, mine):
-        def tell(other):
-            pl.semaphore_signal(barrier, inc=1, device_id=device(other), device_id_type=MESH)
-
-        each(tell)
-
-    greet(*in_xz)
-    greet(*in_group)
+    for flip in (1, 0):
+        for i in range(nz):
+            if flip or i < nz - 1:
+                move = (nz // 2 + (i + 1) // 2 * (1 if i % 2 else -1)) % nz
+                tell(xz_device, lax.rem(x_hi + flip, 2) * nz + lax.rem(z + move, nz))
+    for i in range(1, group):
+        tell(group_device, lax.rem(member + i, group))
+    for load in loads[:5]:
+        load.start()
     for load in loads[:5]:
         load.wait()
 
@@ -338,6 +342,7 @@
     low = near_lane < lanes // 2
     even = lax.rem(lax.div(near_lane, levels), 2) == 0
 
+    stores = []
     for j in range(2):
         recv_all(j, *stage_b)
         four = recv_b[j].reshape(part_m, lanes).astype(F32)
@@ -375,6 +380,8 @@
         send_c[j] = wave.astype(BF16).reshape(send_c.shape[1:])
         start_all(j, *stage_c)
         turned[j] = leg[j].T
+        stores.append(pltpu.make_async_copy(turned.at[j], turned_hbm.at[j], store_sem.at[j]))
+        stores[j].start()
 
     for j in range(2):
         recv_all(j, *stage_c)
@@ -392,18 +399,41 @@
                         moved = parts[ff] if ff == k else pltpu.roll(parts[ff], (ff - k) % 4 * levels, 1)
                         merged = jnp.where(chunk == ff, moved, merged)
                     rows_f[pl.ds((r * waves + w) * lat + 2 * yy + j, nxz, stride=2 * ny), :] = merged
-    stores = []
     for w in range(waves):
-        wave = [rows_f[pl.ds((r * waves + w) * lat, lat), :].astype(BF16) for r in range(2)]
-        out[w] = dot(turned[w], jnp.concatenate(wave, axis=1)).astype(BF16)
-        stores.append(pltpu.make_async_copy(out.at[w], out_hbm.at[w], store_sem.at[w]))
-        stores[w].start()
+        for r in range(2):
+            rows = rows_f[pl.ds((r * waves + w) * lat, lat), :]
+            wave_ref[w, :, pl.ds(r * lanes, lanes)] = rows.astype(BF16)
+        stores.append(pltpu.make_async_copy(wave_ref.at[w], wave_hbm.at[w], store_sem.at[waves + w]))
+        stores[waves + w].start()
 
     send_done(0, *obs_xz)
     send_done(0, *obs_y)
     for j in range(2):
         for stage in (stage_a, stage_b, stage_c, stage_d):
             send_done(j, *stage)
+    for store in stores:
+        store.wait()
+
+
+def finish(cuts, wave_hbm, turned_hbm, out_hbm, wave, turned, out, wave_sem, load_sem, store_sem):
+    waves, nn = turned.shape[0], turned.shape[1]
+    size = nn // cuts
+    wave_loads, loads, stores = [], [], []
+    for w in range(waves):
+        wave_loads.append(pltpu.make_async_copy(wave_hbm.at[w], wave.at[w], wave_sem.at[w]))
+        wave_loads[w].start()
+        for c in range(cuts):
+            i, rows = w * cuts + c, pl.ds(c * size, size)
+            loads.append(pltpu.make_async_copy(turned_hbm.at[w, rows], turned.at[w, rows], load_sem.at[i]))
+            stores.append(pltpu.make_async_copy(out.at[w, rows], out_hbm.at[w, rows], store_sem.at[i]))
+            loads[i].start()
+    for w in range(waves):
+        wave_loads[w].wait()
+        for c in range(cuts):
+            i, rows = w * cuts + c, pl.ds(c * size, size)
+            loads[i].wait()
+            out[w, rows] = dot(turned[w, rows], wave[w]).astype(BF16)
+            stores[i].start()
     for store in stores:
         store.wait()
 
@@ -429,7 +459,7 @@
     hbm = pl.BlockSpec(memory_space=pltpu.HBM)
     band_shape = (vcoef.shape[1], 1, levels)
     scratch = [
-        buffer(waves, nn, width), buffer(waves, nn, lat),
+        buffer(waves, lat, width), buffer(waves, nn, lat),
         buffer(waves, lat, nn), buffer(waves, nn, width), pltpu.VMEM(band_shape, F32),
         buffer(levels, obs_dev), pltpu.VMEM((levels, obs_dev), F32), pltpu.VMEM((1, obs_dev), jnp.int32),
         pltpu.VMEM((1, obs_dev), jnp.int32), pltpu.VMEM((2 * waves * lat, lanes), F32),
@@ -442,15 +472,18 @@
         buffer(2, group, nxz, lanes), buffer(2, group, nxz, lanes),
         pltpu.VMEM((2, slots, lanes), F32), pltpu.VMEM((2, 8, slots), F32),
         buffer(2 * slots, part_m), pltpu.VMEM((2 * slots, 2 * lanes), F32), buffer(part_m, 2 * slots),
-        pltpu.SemaphoreType.DMA((7,)), pltpu.SemaphoreType.DMA((waves,)),
+        pltpu.SemaphoreType.DMA((7,)), pltpu.SemaphoreType.DMA((2 * waves,)),
     ]
     for parts in (2, 2, 1, 1, 2, 2):
         scratch += [pltpu.SemaphoreType.DMA((parts,)), pltpu.SemaphoreType.DMA((parts,))]
-    return pl.pallas_call(
+    wave, turned = pl.pallas_call(
         functools.partial(kernel, nblk, nfld, ny),
-        out_shape=jax.ShapeDtypeStruct((waves, nn, width), BF16),
+        out_shape=(
+            jax.ShapeDtypeStruct((waves, lat, width), BF16),
+            jax.ShapeDtypeStruct((waves, nn, lat), BF16),
+        ),
         in_specs=[hbm] * 7 + [pl.BlockSpec(memory_space=pltpu.SMEM)],
-        out_specs=hbm,
+        out_specs=(hbm, hbm),
         scratch_shapes=scratch,
         compiler_params=pltpu.CompilerParams(
             collective_id=0, has_side_effects=True, vmem_limit_bytes=60 * 1024 * 1024
@@ -459,6 +492,20 @@
         leg, coef, vcoef.reshape(band_shape), obs_value[0], obs_weight[0], obs_dest.reshape(1, obs_dev),
         obs_spot.reshape(1, obs_dev), obs_count,
     )
+    cuts = 2
+    return pl.pallas_call(
+        functools.partial(finish, cuts),
+        out_shape=jax.ShapeDtypeStruct((waves, nn, width), BF16),
+        in_specs=[hbm, hbm],
+        out_specs=hbm,
+        scratch_shapes=[
+            buffer(waves, lat, width), buffer(waves, nn, lat), buffer(waves, nn, width),
+            pltpu.SemaphoreType.DMA((waves,)), pltpu.SemaphoreType.DMA((waves * cuts,)),
+            pltpu.SemaphoreType.DMA((waves * cuts,)),
+        ],
+        compiler_params=pltpu.CompilerParams(vmem_limit_bytes=60 * 1024 * 1024),
+    )(wave, turned)
+
 
 def solution(mesh):
     in_specs = (

time: 62.2 us -> 61.9 us (level)
  local copies, waits for them, and re-layouts: 2.46 us -> 0 us
  Pallas kernels: 58.9 us -> 61.1 us
    unnamed x1 -> x0, local copies, waits for them, and re-layouts: 2.46 us -> none
    pallas_call x1 -> x2, Pallas kernels: 58.9 us -> 61.1 us  [the longest x1 57.9 us: on_device(): pl.pallas_call(functools.partial(kernel, nblk, nfld, ny), out_shape=(jax....]
where the time goes in v4:
time: 61.9 us; the launch traced here: 61.7 us
  Pallas kernels  61.1 us (99%)
  between operations  0.66 us (1%)
    pallas_call x1, Pallas kernels, on_device(): pl.pallas_call(functools.partial(kernel, nblk, nfld, ny), out_shape=(jax....  57.9 us
    pallas_call x1, Pallas kernels, on_device(): pl.pallas_call(functools.partial(finish, cuts), out_shape=jax.ShapeDtypeS...  3.2 us

profile of v4, /device:TPU:1, one launch (start us, length us, event | category | flops | bytes accessed | tf_op | source)
XLA Modules:
  0.0 61.7 jit_solution(3148294366394671498)
XLA Ops:
  0.7 57.9 %shard_map.82 = (bf16[2,256,256]{2,1,0:T(8,128)(2,1)}, bf16[2,1280,256]{2,1,0:T(8,128)(2,1)}) custom-call(bf16[2,256,1280]{2,1,0:T(8,128)(2,1)} %leg_hbm.1, bf16[2,1280,256]{2,1,0:T(8,128)(2,1)} %coef_hbm.1, f32[7,1,32]{2,1,0:T(1,128)} %bitcast.7, bf16[32,512]{1,0:T(8,128)(2,1)} %bitcast.6, f32[32,512]{1,0:T(8,128)} %bitcast.5, s32[1,512]{1,0:T(1,128)} %bitcast.8, ...), custom_call_target="tpu_custom_call" | custom-call | tf_op jit(solution)/shard_map/pallas_call | solution.py:479
  58.5 3.2 %shard_map.83 = bf16[2,1280,256]{2,1,0:T(8,128)(2,1)} custom-call(bf16[2,256,256]{2,1,0:T(8,128)(2,1)} %get-tuple-element.7.wave_hbm, bf16[2,1280,256]{2,1,0:T(8,128)(2,1)} %get-tuple-element.8.turned_hbm), custom_call_target="tpu_custom_call" | custom-call | tf_op jit(solution)/shard_map/pallas_call | solution.py:496
